TPU v7x, 32 devices: a whole 2x2x4 slice. The times are simulated.
32 devices in a mesh: gx: 4 (over z), gy: 8 (over y, x, core).
Axes of the slice: x: 2, y: 2, z: 4, core: 2. Of those that a mesh axis runs over, the one named last changes fastest.
Arguments:
- velocity: float32 [3, 384, 128, 128], P(None, 'gx', 'gy'), may hold values from -6 to 6
- states: float32 [2, 384, 128, 128], P(None, 'gx', 'gy'), may hold values from -6 to 6
- pull_plan: int32 [24, 8], P('gx', 'gy'), may hold values from 0 to 15, as said below
- send_plan: int32 [4, 8, 8, 2], P('gx', 'gy'), may hold values from -1 to 5, as said below
- codes: int32 [3, 24, 8], P(None, 'gx', 'gy'), may hold values from 0 to 1023, as said below
Outputs:
- hessian_velocity: float32 [3, 384, 128, 128], P(None, 'gx', 'gy')
Inputs may be any that keep to these rules, and one draw needn't show every extreme that they name: `pull_plan`: the bricks of one device name distinct slots; slot p of device (g, h) is filled by device (g, p // 2) along gy. Every device uses 2 slots from at least one supplying device, and at most 2 from any. send_plan[g, s, h, e] is the brick of device (g, s), in order of brick rows then brick columns within the device, that fills slot s * 2 + e of device (g, h), or -1 where no brick of device (g, h) names that slot; it agrees with pull_plan. codes[0] and codes[1] lie in 0 .. 7; codes[2] is the depth position in units of 1 / 8 cell.
All inputs are finite; a program needn't handle non-finite values.
Results may differ from a plain program's by a relative error of at most 0.00013.
Values sent between devices are 32-bit elements; how exact they have to be, the bound alone decides.
A program may use at most 128 MiB of HBM per device.

v0:
```python
import jax
import jax.numpy as jnp
from jax import lax
from jax.sharding import PartitionSpec as P

BX = 16
BY = 16
CAP = 2
QF = 8
STEPS = 2


def with_halo(cells, sides, width):
    for axis, dim in sides:
        count = lax.axis_size(axis)
        head = lax.slice_in_dim(cells, 0, width, axis=dim)
        tail = lax.slice_in_dim(cells, cells.shape[dim] - width, cells.shape[dim], axis=dim)
        cells = jnp.concatenate(
            [
                lax.ppermute(tail, axis, [(i, (i + 1) % count) for i in range(count)]),
                cells,
                lax.ppermute(head, axis, [((i + 1) % count, i) for i in range(count)]),
            ],
            axis=dim,
        )
    return cells


def cubic_weights(fraction):
    return (
        -fraction * (fraction - 1.0) * (fraction - 2.0) / 6.0,
        (fraction + 1.0) * (fraction - 1.0) * (fraction - 2.0) / 2.0,
        -(fraction + 1.0) * fraction * (fraction - 2.0) / 2.0,
        (fraction + 1.0) * fraction * (fraction - 1.0) / 6.0,
    )


def band_matrix(code_row, cells):
    fraction = code_row.astype(jnp.float32) / QF
    weights = cubic_weights(fraction[:, None, None])
    row_index = jnp.arange(cells)[None, :, None]
    col_index = jnp.arange(cells + 3)[None, None, :]
    total = jnp.zeros((code_row.shape[0], cells, cells + 3), jnp.float32)
    for offset in range(4):
        total = total + weights[offset] * (col_index == row_index + offset).astype(jnp.float32)
    return total


def circulant(code_row, cells):
    shift_cells = code_row // QF
    fraction = (code_row % QF).astype(jnp.float32) / QF
    weights = cubic_weights(fraction[:, None, None])
    row_index = jnp.arange(cells)[None, :, None]
    col_index = jnp.arange(cells)[None, None, :]
    total = jnp.zeros((code_row.shape[0], cells, cells), jnp.float32)
    for offset in range(4):
        target = (row_index + shift_cells[:, None, None] + offset - 1) % cells
        total = total + weights[offset] * (col_index == target).astype(jnp.float32)
    return total


def interpolate(windows, weight_rows, weight_cols, weight_depth):
    high = lax.Precision.HIGHEST
    along_depth = jnp.einsum("nabz,ncz->nabc", windows, weight_depth, precision=high)
    along_rows = jnp.einsum("nia,nabc->nibc", weight_rows, along_depth, precision=high)
    return jnp.einsum("njb,nibc->nijc", weight_cols, along_rows, precision=high)


def interpolate_adjoint(values, weight_rows, weight_cols, weight_depth):
    high = lax.Precision.HIGHEST
    along_cols = jnp.einsum("njb,nijc->nibc", weight_cols, values, precision=high)
    along_rows = jnp.einsum("nia,nibc->nabc", weight_rows, along_cols, precision=high)
    return jnp.einsum("ncz,nabc->nabz", weight_depth, along_rows, precision=high)


def extend(stacked):
    return with_halo(stacked, (("gx", 1), ("gy", 2)), 2)


def cut_windows(extended, brick_rows):
    pieces = []
    for row_brick in range(brick_rows):
        pieces.append(extended[row_brick * BX + 1 : row_brick * BX + BX + 4, 1 : BY + 4])
    return jnp.stack(pieces)


def place_windows(collected, brick_rows, brick_cols, rows_dev, cols_dev, depth_cells):
    accumulate = jnp.zeros((rows_dev + 4, cols_dev + 4, depth_cells), jnp.float32)
    for row_brick in range(brick_rows):
        accumulate = accumulate.at[row_brick * BX + 1 : row_brick * BX + BX + 4, 1 : BY + 4].add(
            collected[row_brick * brick_cols]
        )
    return accumulate


def fold_margins(accumulate, rows_dev, cols_dev, depth_cells):
    strips = jnp.zeros((3, rows_dev, cols_dev, depth_cells), jnp.float32)
    strips = strips.at[0, 0:2].set(accumulate[0:2, 2 : cols_dev + 2])
    strips = strips.at[0, rows_dev - 2 :].set(accumulate[rows_dev + 2 :, 2 : cols_dev + 2])
    strips = strips.at[1, :, 0:2].set(accumulate[2 : rows_dev + 2, 0:2])
    strips = strips.at[1, :, cols_dev - 2 :].set(accumulate[2 : rows_dev + 2, cols_dev + 2 :])
    strips = strips.at[2, 0:2, 0:2].set(accumulate[0:2, 0:2])
    strips = strips.at[2, 0:2, cols_dev - 2 :].set(accumulate[0:2, cols_dev + 2 :])
    strips = strips.at[2, rows_dev - 2 :, 0:2].set(accumulate[rows_dev + 2 :, 0:2])
    strips = strips.at[2, rows_dev - 2 :, cols_dev - 2 :].set(
        accumulate[rows_dev + 2 :, cols_dev + 2 :]
    )
    arrived = with_halo(strips, (("gx", 1), ("gy", 2)), 2)
    result = accumulate[2 : rows_dev + 2, 2 : cols_dev + 2]
    result = result.at[0:2].add(arrived[0, 0:2, 2 : cols_dev + 2])
    result = result.at[rows_dev - 2 :].add(arrived[0, rows_dev + 2 :, 2 : cols_dev + 2])
    result = result.at[:, 0:2].add(arrived[1, 2 : rows_dev + 2, 0:2])
    result = result.at[:, cols_dev - 2 :].add(arrived[1, 2 : rows_dev + 2, cols_dev + 2 :])
    result = result.at[0:2, 0:2].add(arrived[2, 0:2, 0:2])
    result = result.at[0:2, cols_dev - 2 :].add(arrived[2, 0:2, cols_dev + 2 :])
    result = result.at[rows_dev - 2 :, 0:2].add(arrived[2, rows_dev + 2 :, 0:2])
    result = result.at[rows_dev - 2 :, cols_dev - 2 :].add(
        arrived[2, rows_dev + 2 :, cols_dev + 2 :]
    )
    return result


def body(velocity, states, pull_plan, send_plan, codes):
    rows_dev = velocity.shape[1]
    cols_dev = velocity.shape[2]
    depth_cells = velocity.shape[3]
    brick_rows = rows_dev // BX
    brick_cols = cols_dev // BY
    bricks = brick_rows * brick_cols
    peer_count = lax.axis_size("gy")
    slot_count = peer_count * CAP
    step_size = 1.0 / STEPS
    high = lax.Precision.HIGHEST
    pull_flat = pull_plan.reshape(bricks)
    owners = send_plan.reshape(slot_count)
    send_flat = jnp.maximum(owners, 0)
    code_flat = codes.reshape(3, bricks)
    selector = (owners[None, :] == jnp.arange(bricks)[:, None]).astype(jnp.float32)
    request = jnp.zeros((slot_count, 3), jnp.int32).at[pull_flat].set(code_flat.T)
    requested = lax.all_to_all(
        request.reshape(peer_count, CAP, 3), "gy", split_axis=0, concat_axis=0, tiled=True
    ).reshape(slot_count, 3)
    weight_rows = band_matrix(requested[:, 0], BX)
    weight_cols = band_matrix(requested[:, 1], BY)
    weight_depth = circulant(requested[:, 2], depth_cells)
    extended_states = extend(states)
    centre = extended_states[:, 2 : rows_dev + 2, 2 : cols_dev + 2]
    grad_rows = (
        extended_states[:, 3 : rows_dev + 3, 2 : cols_dev + 2]
        - extended_states[:, 1 : rows_dev + 1, 2 : cols_dev + 2]
    ) * 0.5
    grad_cols = (
        extended_states[:, 2 : rows_dev + 2, 3 : cols_dev + 3]
        - extended_states[:, 2 : rows_dev + 2, 1 : cols_dev + 1]
    ) * 0.5
    grad_depth = (jnp.roll(centre, -1, 3) - jnp.roll(centre, 1, 3)) * 0.5
    gradients = jnp.stack([grad_rows, grad_cols, grad_depth], axis=1)
    tangent = jnp.zeros((rows_dev, cols_dev, depth_cells), jnp.float32)
    for step in range(STEPS):
        extended = extend(
            (tangent - step_size * jnp.sum(velocity * gradients[step], axis=0))[None]
        )[0]
        windows = cut_windows(extended, brick_rows)
        supplied = interpolate(
            jnp.take(windows, send_flat, axis=0), weight_rows, weight_cols, weight_depth
        )
        pull_inbox = lax.all_to_all(
            supplied.reshape(peer_count, CAP, BX, BY, depth_cells),
            "gy",
            split_axis=0,
            concat_axis=0,
            tiled=True,
        ).reshape(slot_count, BX, BY, depth_cells)
        tangent = (
            jnp.take(pull_inbox, pull_flat, axis=0)
            .reshape(brick_rows, brick_cols, BX, BY, depth_cells)
            .transpose(0, 2, 1, 3, 4)
            .reshape(rows_dev, cols_dev, depth_cells)
        )
    adjoint = tangent
    force = jnp.zeros((3, rows_dev, cols_dev, depth_cells), jnp.float32)
    for step in reversed(range(STEPS)):
        outbox = (
            jnp.zeros((slot_count, BX, BY, depth_cells), jnp.float32)
            .at[pull_flat]
            .set(
                adjoint.reshape(brick_rows, BX, brick_cols, BY, depth_cells)
                .transpose(0, 2, 1, 3, 4)
                .reshape(bricks, BX, BY, depth_cells)
            )
            .reshape(peer_count, CAP, BX, BY, depth_cells)
        )
        inbox = lax.all_to_all(outbox, "gy", split_axis=0, concat_axis=0, tiled=True).reshape(
            slot_count, BX, BY, depth_cells
        )
        collected = jnp.einsum(
            "ks,sabz->kabz",
            selector,
            interpolate_adjoint(inbox, weight_rows, weight_cols, weight_depth),
            precision=high,
        )
        accumulate = place_windows(
            collected, brick_rows, brick_cols, rows_dev, cols_dev, depth_cells
        )
        adjoint = fold_margins(accumulate, rows_dev, cols_dev, depth_cells)
        force = force - step_size * adjoint[None] * gradients[step]
    return force


def solution(mesh):
    return jax.shard_map(
        body,
        mesh=mesh,
        in_specs=(
            P(None, "gx", "gy", None),
            P(None, "gx", "gy", None),
            P("gx", "gy"),
            P("gx", "gy", None, None),
            P(None, "gx", "gy"),
        ),
        out_specs=P(None, "gx", "gy", None),
        check_vma=False,
    )
```

profile of v0, /device:TPU:0, one launch (start us, length us, event | category | flops | bytes accessed | tf_op | source)
XLA Modules:
  0.0 325.2 jit_solution(679404109927343971)
XLA Ops:
  0.8 3.0 collective-permute-start.1
  8.5 3.9 %all-to-all-start = ((s32[8,2,3]{2,1,0:T(2,128)}), s32[8,2,3]{2,1,0:T(2,128)S(1)}, u32[]{:S(2)}, u32[]{:S(2)}) async-start(s32[8,2,3]{2,1,0:T(2,128)} %bitcast.4), calls=%async_computation | async-start | bytes 16384 | tf_op jit(solution)/shard_map/all_to_all | solution.py:140
  12.4 3.8 %fusion.228 = (f32[2,96,16,1]{3,2,1,0:T(8,128)S(1)}, f32[2,96,16,1]{3,2,1,0:T(8,128)}) fusion(f32[2,96,16,128]{3,2,1,0:T(8,128)} %param.98), kind=kLoop, calls=%fused_computation.425 | loop fusion | bytes 49152 | tf_op jit(solution)/shard_map/jit(_roll_static)/slice | solution.py:156
  24.8 3.7 %fusion.22 = f32[2,1,96,16,128]{4,3,2,1,0:T(8,128)S(1)} fusion(f32[2,1,96,16,1]{4,3,2,1,0:T(8,128)} %copy.48, f32[2,1,96,16,127]{4,3,2,1,0:T(8,128)} %get-tuple-element.556, f32[2,1,96,16,127]{4,3,2,1,0:T(8,128)} %get-tuple-element.555, f32[2,1,96,16,1]{4,3,2,1,0:T(8,128)} %copy.50), kind=kLoop, calls=%fused_computation.44 | loop fusion | flops 1572864 | bytes 4718592 | tf_op jit(solution)/shard_map/mul | solution.py:156
  32.3 4.3 %collective-permute-done.2 = f32[2,100,2,128]{3,2,1,0:T(2,128)S(1)} collective-permute-done((f32[2,100,2,128]{3,2,1,0:T(2,128)S(1)}, f32[2,100,2,128]{3,2,1,0:T(2,128)S(1)}, u32[]{:S(2)}, u32[]{:S(2)}) %collective-permute-start.2) | collective-permute-done | bytes 204832 | tf_op jit(solution)/shard_map/ppermute | solution.py:22
  43.3 3.8 %collective-permute-start.5 = (f32[1,2,16,128]{3,2,1,0:T(8,128)S(1)}, f32[1,2,16,128]{3,2,1,0:T(8,128)S(1)}, u32[]{:S(2)}, u32[]{:S(2)}) collective-permute-start(f32[1,2,16,128]{3,2,1,0:T(8,128)S(1)} %get-tuple-element.576), channel_id=1, source_target_pairs={{8,0},{16,8},{24,16},{0,24},{9,1},{17,9},{25,17},{1,25},{10,2},{18... | collective-permute-start | bytes 49160 | tf_op jit(solution)/shard_map/ppermute | solution.py:22
  49.0 2.8 collective-permute-start.7
  59.5 8.8 %fusion.2 = f32[16,19,19,128]{3,1,2,0:T(8,128)S(1)} fusion(f32[16,19,19,128]{3,2,1,0:T(8,128)S(1)} %broadcast_select_fusion.1, f32[16]{0:T(128)S(1)} %get-tuple-element.596, s32[16,128]{1,0:T(8,128)S(1)} %get-tuple-element.593, f32[16]{0:T(128)S(1)} %get-tuple-element.597, s32[16,128]{1,0:T(8,128)S(1)} %get-tuple-element.592, ...), kind=kOutput, calls=%fused_computation.10 | convolution fusion | flops 1138491392 | bytes 5947648 | tf_op jit(solution)/shard_map/nabz,ncz->nabc/dot_general | solution.py:64
  71.0 4.3 %fusion.6 = f32[16,16,128,16]{2,3,1,0:T(8,128)} fusion(f32[16,16,19,128]{3,1,2,0:T(8,128)S(1)} %fusion.87, f32[16]{0:T(128)S(1)} %get-tuple-element.586, f32[16]{0:T(128)S(1)} %get-tuple-element.585, f32[16]{0:T(128)S(1)} %get-tuple-element.584, f32[16]{0:T(128)S(1)} %get-tuple-element.583, f32[16,19]{1,0:T(8,128)S(1)} %fusion.187, ...), kind=kOutput, calls=%fused_computation.14 | convolution fusion | flops 119571712 | bytes 4592640 | tf_op jit(solution)/shard_map/njb,nibc->nijc/dot_general | solution.py:66
  75.3 4.1 %all-to-all-start.1 = ((f32[8,2,16,16,128]{4,3,2,1,0:T(8,128)}), f32[8,2,16,16,128]{4,3,2,1,0:T(8,128)S(1)}, u32[]{:S(2)}, u32[]{:S(2)}) async-start(f32[8,2,16,16,128]{4,3,2,1,0:T(8,128)} %bitcast.34), calls=%async_computation.1 | async-start | bytes 4194304 | tf_op jit(solution)/shard_map/all_to_all | solution.py:167
  79.5 26.6 %all-to-all-done.1 = f32[8,2,16,16,128]{4,3,2,1,0:T(8,128)S(1)} async-done(((f32[8,2,16,16,128]{4,3,2,1,0:T(8,128)}), f32[8,2,16,16,128]{4,3,2,1,0:T(8,128)S(1)}, u32[]{:S(2)}, u32[]{:S(2)}) %all-to-all-start.1) | async-done | bytes 2097184 | tf_op jit(solution)/shard_map/all_to_all | solution.py:167
  109.0 3.9 %collective-permute-start.9 = (f32[1,2,16,128]{3,2,1,0:T(8,128)S(1)}, f32[1,2,16,128]{3,2,1,0:T(8,128)S(1)}, u32[]{:S(2)}, u32[]{:S(2)}) collective-permute-start(f32[1,2,16,128]{3,2,1,0:T(8,128)S(1)} %get-tuple-element.574), channel_id=1, source_target_pairs={{8,0},{16,8},{24,16},{0,24},{9,1},{17,9},{25,17},{1,25},{10,2},{18... | collective-permute-start | bytes 49160 | tf_op jit(solution)/shard_map/ppermute | solution.py:22
  114.7 2.9 collective-permute-start.11
  117.6 3.0 collective-permute-done.10
  126.0 8.8 %fusion = f32[16,19,19,128]{3,1,2,0:T(8,128)S(1)} fusion(f32[16,19,19,128]{3,2,1,0:T(8,128)S(1)} %broadcast_select_fusion, f32[16]{0:T(128)S(1)} %get-tuple-element.596, s32[16,128]{1,0:T(8,128)S(1)} %get-tuple-element.593, f32[16]{0:T(128)S(1)} %get-tuple-element.597, s32[16,128]{1,0:T(8,128)S(1)} %get-tuple-element.592, f32[16]{0:T(128)S(1)} %get-tuple-element.595, ...), kind=kOutput, calls=%fused_computation.8 | convolution fusion | flops 1138491392 | bytes 5947648 | tf_op jit(solution)/shard_map/nabz,ncz->nabc/dot_general | solution.py:64
  137.5 3.0 fusion.4
  140.5 29.7 %all_to_all.25 = f32[8,2,16,16,128]{4,3,2,1,0:T(8,128)S(1)} all-to-all(f32[8,2,16,16,128]{4,3,2,1,0:T(8,128)S(1)} %bitcast.467), channel_id=1, replica_groups=mesh['gx'=4,'gy'=8] {'gy'}, dimensions={0} | all-to-all | bytes 4194304 | tf_op jit(solution)/shard_map/all_to_all | solution.py:167
  172.5 2.7 scatter_fusion
  175.2 4.2 %all-to-all-start.3 = ((f32[8,2,16,16,128]{4,3,2,1,0:T(8,128)}), f32[8,2,16,16,128]{4,3,2,1,0:T(8,128)S(1)}, u32[]{:S(2)}, u32[]{:S(2)}) async-start(f32[8,2,16,16,128]{4,3,2,1,0:T(8,128)} %bitcast.49), calls=%async_computation.3 | async-start | bytes 4194304 | tf_op jit(solution)/shard_map/all_to_all | solution.py:193
  181.5 24.5 %all-to-all-done.3 = f32[8,2,16,16,128]{4,3,2,1,0:T(8,128)S(1)} async-done(((f32[8,2,16,16,128]{4,3,2,1,0:T(8,128)}), f32[8,2,16,16,128]{4,3,2,1,0:T(8,128)S(1)}, u32[]{:S(2)}, u32[]{:S(2)}) %all-to-all-start.3) | async-done | bytes 2097184 | tf_op jit(solution)/shard_map/all_to_all | solution.py:193
  206.0 3.2 convolution_bitcast_fusion.1
  209.2 3.9 %fusion.14 = f32[16,19,19,128]{3,1,2,0:T(8,128)S(1)} fusion(f32[16,16,19,128]{3,2,1,0:T(8,128)S(1)} %convolution_bitcast_fusion.1, f32[16,19]{1,0:T(8,128)S(1)} %fusion.187, f32[16]{0:T(128)S(1)} %get-tuple-element.590, f32[16,19]{1,0:T(8,128)S(1)} %get-tuple-element.601, f32[16]{0:T(128)S(1)} %get-tuple-element.589, f32[16,19]{1,0:T(8,128)S(1)} %fusion.185, ...), kind=kOutput, calls=%fused_computation.22 | convolution fusion | flops 141985024 | bytes 5452800 | tf_op jit(solution)/shard_map/nia,nibc->nabc/dot_general | solution.py:72
  213.1 8.8 %fusion.25 = f32[16,19,19,128]{3,1,2,0:T(8,128)S(1)} fusion(f32[16,19,19,128]{3,1,2,0:T(8,128)S(1)} %fusion.14, f32[16]{0:T(128)S(1)} %get-tuple-element.596, s32[16,128]{1,0:T(8,128)S(1)} %get-tuple-element.593, f32[16]{0:T(128)S(1)} %get-tuple-element.597, s32[16,128]{1,0:T(8,128)S(1)} %get-tuple-element.592, f32[16]{0:T(128)S(1)} %get-tuple-element.595, ...), kind=kOutput, calls=%fused_computation.51 | convolution fusion | flops 1138491392 | bytes 5947648 | tf_op jit(solution)/shard_map/ncz,nabc->nabz/dot_general | solution.py:73
  229.2 2.8 collective-permute-start.13
  234.3 2.8 collective-permute-start.15
  237.1 7.4 %collective-permute-done.14 = f32[3,100,2,128]{3,2,1,0:T(2,128)S(1)} collective-permute-done((f32[3,100,2,128]{3,2,1,0:T(2,128)S(1)}, f32[3,100,2,128]{3,2,1,0:T(2,128)S(1)}, u32[]{:S(2)}, u32[]{:S(2)}) %collective-permute-start.14) | collective-permute-done | bytes 307232 | tf_op jit(solution)/shard_map/ppermute | solution.py:20
  249.1 29.0 %all_to_all.26 = f32[8,2,16,16,128]{4,3,2,1,0:T(8,128)S(1)} all-to-all(f32[8,2,16,16,128]{4,3,2,1,0:T(8,128)S(1)} %bitcast.463), channel_id=1, replica_groups=mesh['gx'=4,'gy'=8] {'gy'}, dimensions={0} | all-to-all | bytes 4194304 | tf_op jit(solution)/shard_map/all_to_all | solution.py:193
  278.2 3.2 convolution_bitcast_fusion
  281.4 3.9 %fusion.12 = f32[16,19,19,128]{3,1,2,0:T(8,128)S(1)} fusion(f32[16,16,19,128]{3,2,1,0:T(8,128)S(1)} %convolution_bitcast_fusion, f32[16,19]{1,0:T(8,128)S(1)} %fusion.187, f32[16]{0:T(128)S(1)} %get-tuple-element.590, f32[16,19]{1,0:T(8,128)S(1)} %get-tuple-element.601, f32[16]{0:T(128)S(1)} %get-tuple-element.589, f32[16,19]{1,0:T(8,128)S(1)} %fusion.185, ...), kind=kOutput, calls=%fused_computation.20 | convolution fusion | flops 141985024 | bytes 5452800 | tf_op jit(solution)/shard_map/nia,nibc->nabc/dot_general | solution.py:72
  285.2 8.8 %fusion.23 = f32[16,19,19,128]{3,1,2,0:T(8,128)S(1)} fusion(f32[16,19,19,128]{3,1,2,0:T(8,128)S(1)} %fusion.12, f32[16]{0:T(128)S(1)} %get-tuple-element.596, s32[16,128]{1,0:T(8,128)S(1)} %get-tuple-element.593, f32[16]{0:T(128)S(1)} %get-tuple-element.597, s32[16,128]{1,0:T(8,128)S(1)} %get-tuple-element.592, f32[16]{0:T(128)S(1)} %get-tuple-element.595, ...), kind=kOutput, calls=%fused_computation.49 | convolution fusion | flops 1138491392 | bytes 5947648 | tf_op jit(solution)/shard_map/ncz,nabc->nabz/dot_general | solution.py:73
  309.8 7.3 %collective-permute-done.18 = f32[3,100,2,128]{3,2,1,0:T(2,128)S(1)} collective-permute-done((f32[3,100,2,128]{3,2,1,0:T(2,128)S(1)}, f32[3,100,2,128]{3,2,1,0:T(2,128)S(1)}, u32[]{:S(2)}, u32[]{:S(2)}) %collective-permute-start.18) | collective-permute-done | bytes 307232 | tf_op jit(solution)/shard_map/ppermute | solution.py:20
  320.8 4.2 %multiply_subtract_fusion = f32[3,96,16,128]{3,2,1,0:T(8,128)} fusion(f32[2,3,96,16,128]{4,3,2,1,0:T(8,128)} %copy-done, f32[96,16,128]{2,1,0:T(8,128)S(1)} %multiply_bitcast_fusion, f32[96,16,128]{2,1,0:T(8,128)S(1)} %broadcast_multiply_fusion), kind=kLoop, calls=%fused_computation.26 | loop fusion | flops 2359296 | bytes 8650752 | tf_op jit(solution)/shard_map/sub | solution.py:206
  (201 shorter events, 87.0 us)
Async XLA Ops:
  0.8 28.4 %collective-permute-start.1 = (f32[2,2,16,128]{3,2,1,0:T(8,128)S(1)}, f32[2,2,16,128]{3,2,1,0:T(8,128)S(1)}, u32[]{:S(2)}, u32[]{:S(2)}) collective-permute-start(f32[2,2,16,128]{3,2,1,0:T(8,128)S(1)} %get-tuple-element.552), channel_id=1, source_target_pairs={{0,8},{8,16},{16,24},{24,0},{1,9},{9,17},{17,25},{25,1},{2,10},{10... | collective-permute-start | bytes 98312 | tf_op jit(solution)/shard_map/ppermute | solution.py:20
  3.8 25.4 %collective-permute-start = (f32[2,2,16,128]{3,2,1,0:T(8,128)S(1)}, f32[2,2,16,128]{3,2,1,0:T(8,128)S(1)}, u32[]{:S(2)}, u32[]{:S(2)}) collective-permute-start(f32[2,2,16,128]{3,2,1,0:T(8,128)S(1)} %get-tuple-element.551), channel_id=1, source_target_pairs={{8,0},{16,8},{24,16},{0,24},{9,1},{17,9},{25,17},{1,25},{10,2},{18... | collective-permute-start | bytes 98312 | tf_op jit(solution)/shard_map/ppermute | solution.py:22
  6.5 165.9 %copy-start.3 = (s32[6]{0:T(128)}, s32[6]{0:T(128)S(1)}, u32[]{:S(2)}) copy-start(s32[6]{0:T(128)S(1)} %fusion.204) | copy-start | bytes 76
  8.5 20.1 %all-to-all-start = ((s32[8,2,3]{2,1,0:T(2,128)}), s32[8,2,3]{2,1,0:T(2,128)S(1)}, u32[]{:S(2)}, u32[]{:S(2)}) async-start(s32[8,2,3]{2,1,0:T(2,128)} %bitcast.4), calls=%async_computation | async-start | bytes 16384 | tf_op jit(solution)/shard_map/all_to_all | solution.py:140
  12.4 3.8 %copy-start.1 = (f32[2,96,16,128]{3,2,1,0:T(8,128)S(1)}, f32[2,96,16,128]{3,2,1,0:T(8,128)}, u32[]{:S(2)}) copy-start(f32[2,96,16,128]{3,2,1,0:T(8,128)} %param.98) | copy-start | bytes 4718596
  16.2 2.2 copy-start.5
  29.6 7.1 %collective-permute-start.2 = (f32[2,100,2,128]{3,2,1,0:T(2,128)S(1)}, f32[2,100,2,128]{3,2,1,0:T(2,128)S(1)}, u32[]{:S(2)}, u32[]{:S(2)}) collective-permute-start(f32[2,100,2,128]{3,2,1,0:T(2,128)S(1)} %get-tuple-element.547), channel_id=1, source_target_pairs={{1,0},{2,1},{3,2},{4,3},{5,4},{6,5},{7,6},{0,7},{9,8},{10,9},{11,1... | collective-permute-start | bytes 614408 | tf_op jit(solution)/shard_map/ppermute | solution.py:22
  32.3 6.5 %collective-permute-start.3 = (f32[2,100,2,128]{3,2,1,0:T(2,128)S(1)}, f32[2,100,2,128]{3,2,1,0:T(2,128)S(1)}, u32[]{:S(2)}, u32[]{:S(2)}) collective-permute-start(f32[2,100,2,128]{3,2,1,0:T(2,128)S(1)} %get-tuple-element.548), channel_id=1, source_target_pairs={{0,1},{1,2},{2,3},{3,4},{4,5},{5,6},{6,7},{7,0},{8,9},{9,10},{10,1... | collective-permute-start | bytes 614408 | tf_op jit(solution)/shard_map/ppermute | solution.py:20
  39.4 1.7 copy-start.2
  41.0 2.1 copy-start
  43.2 5.6 %collective-permute-start.4 = (f32[1,2,16,128]{3,2,1,0:T(8,128)S(1)}, f32[1,2,16,128]{3,2,1,0:T(8,128)S(1)}, u32[]{:S(2)}, u32[]{:S(2)}) collective-permute-start(f32[1,2,16,128]{3,2,1,0:T(8,128)S(1)} %get-tuple-element.575), channel_id=1, source_target_pairs={{0,8},{8,16},{16,24},{24,0},{1,9},{9,17},{17,25},{25,1},{2,10},{10... | collective-permute-start | bytes 49160 | tf_op jit(solution)/shard_map/ppermute | solution.py:20
  43.3 5.5 %collective-permute-start.5 = (f32[1,2,16,128]{3,2,1,0:T(8,128)S(1)}, f32[1,2,16,128]{3,2,1,0:T(8,128)S(1)}, u32[]{:S(2)}, u32[]{:S(2)}) collective-permute-start(f32[1,2,16,128]{3,2,1,0:T(8,128)S(1)} %get-tuple-element.576), channel_id=1, source_target_pairs={{8,0},{16,8},{24,16},{0,24},{9,1},{17,9},{25,17},{1,25},{10,2},{18... | collective-permute-start | bytes 49160 | tf_op jit(solution)/shard_map/ppermute | solution.py:22
  48.9 5.1 %collective-permute-start.6 = (f32[1,100,2,128]{3,2,1,0:T(2,128)S(1)}, f32[1,100,2,128]{3,2,1,0:T(2,128)S(1)}, u32[]{:S(2)}, u32[]{:S(2)}) collective-permute-start(f32[1,100,2,128]{3,2,1,0:T(2,128)S(1)} %get-tuple-element.571), channel_id=1, source_target_pairs={{0,1},{1,2},{2,3},{3,4},{4,5},{5,6},{6,7},{7,0},{8,9},{9,10},{10,1... | collective-permute-start | bytes 307208 | tf_op jit(solution)/shard_map/ppermute | solution.py:20
  49.0 5.1 %collective-permute-start.7 = (f32[1,100,2,128]{3,2,1,0:T(2,128)S(1)}, f32[1,100,2,128]{3,2,1,0:T(2,128)S(1)}, u32[]{:S(2)}, u32[]{:S(2)}) collective-permute-start(f32[1,100,2,128]{3,2,1,0:T(2,128)S(1)} %get-tuple-element.572), channel_id=1, source_target_pairs={{1,0},{2,1},{3,2},{4,3},{5,4},{6,5},{7,6},{0,7},{9,8},{10,9},{11,1... | collective-permute-start | bytes 307208 | tf_op jit(solution)/shard_map/ppermute | solution.py:22
  75.3 4.1 %copy-start.8 = (s32[6,1]{0,1:T(1,128)S(1)}, s32[6,1]{0,1:T(1,128)}, u32[]{:S(2)}) copy-start(s32[6,1]{0,1:T(1,128)} %param.99) | copy-start | bytes 76
  75.3 30.8 %all-to-all-start.1 = ((f32[8,2,16,16,128]{4,3,2,1,0:T(8,128)}), f32[8,2,16,16,128]{4,3,2,1,0:T(8,128)S(1)}, u32[]{:S(2)}, u32[]{:S(2)}) async-start(f32[8,2,16,16,128]{4,3,2,1,0:T(8,128)} %bitcast.34), calls=%async_computation.1 | async-start | bytes 4194304 | tf_op jit(solution)/shard_map/all_to_all | solution.py:167
  108.9 5.6 %collective-permute-start.8 = (f32[1,2,16,128]{3,2,1,0:T(8,128)S(1)}, f32[1,2,16,128]{3,2,1,0:T(8,128)S(1)}, u32[]{:S(2)}, u32[]{:S(2)}) collective-permute-start(f32[1,2,16,128]{3,2,1,0:T(8,128)S(1)} %get-tuple-element.573), channel_id=1, source_target_pairs={{0,8},{8,16},{16,24},{24,0},{1,9},{9,17},{17,25},{25,1},{2,10},{10... | collective-permute-start | bytes 49160 | tf_op jit(solution)/shard_map/ppermute | solution.py:20
  109.0 5.5 %collective-permute-start.9 = (f32[1,2,16,128]{3,2,1,0:T(8,128)S(1)}, f32[1,2,16,128]{3,2,1,0:T(8,128)S(1)}, u32[]{:S(2)}, u32[]{:S(2)}) collective-permute-start(f32[1,2,16,128]{3,2,1,0:T(8,128)S(1)} %get-tuple-element.574), channel_id=1, source_target_pairs={{8,0},{16,8},{24,16},{0,24},{9,1},{17,9},{25,17},{1,25},{10,2},{18... | collective-permute-start | bytes 49160 | tf_op jit(solution)/shard_map/ppermute | solution.py:22
  114.6 5.9 %collective-permute-start.10 = (f32[1,100,2,128]{3,2,1,0:T(2,128)S(1)}, f32[1,100,2,128]{3,2,1,0:T(2,128)S(1)}, u32[]{:S(2)}, u32[]{:S(2)}) collective-permute-start(f32[1,100,2,128]{3,2,1,0:T(2,128)S(1)} %get-tuple-element.569), channel_id=1, source_target_pairs={{0,1},{1,2},{2,3},{3,4},{4,5},{5,6},{6,7},{7,0},{8,9},{9,10},{10,1... | collective-permute-start | bytes 307208 | tf_op jit(solution)/shard_map/ppermute | solution.py:20
  114.7 5.8 %collective-permute-start.11 = (f32[1,100,2,128]{3,2,1,0:T(2,128)S(1)}, f32[1,100,2,128]{3,2,1,0:T(2,128)S(1)}, u32[]{:S(2)}, u32[]{:S(2)}) collective-permute-start(f32[1,100,2,128]{3,2,1,0:T(2,128)S(1)} %get-tuple-element.570), channel_id=1, source_target_pairs={{1,0},{2,1},{3,2},{4,3},{5,4},{6,5},{7,6},{0,7},{9,8},{10,9},{11,1... | collective-permute-start | bytes 307208 | tf_op jit(solution)/shard_map/ppermute | solution.py:22
  175.2 4.8 %copy-start.7 = (s32[3]{0:T(128)S(1)}, s32[3]{0:T(128)}, u32[]{:S(2)}) copy-start(s32[3]{0:T(128)} %constant.1251.clone.1) | copy-start | bytes 40
  175.2 5.6 %copy-start.6 = (s32[4]{0:T(128)S(1)}, s32[4]{0:T(128)}, u32[]{:S(2)}) copy-start(s32[4]{0:T(128)} %constant.1248.clone.1) | copy-start | bytes 52
  175.2 30.8 %all-to-all-start.3 = ((f32[8,2,16,16,128]{4,3,2,1,0:T(8,128)}), f32[8,2,16,16,128]{4,3,2,1,0:T(8,128)S(1)}, u32[]{:S(2)}, u32[]{:S(2)}) async-start(f32[8,2,16,16,128]{4,3,2,1,0:T(8,128)} %bitcast.49), calls=%async_computation.3 | async-start | bytes 4194304 | tf_op jit(solution)/shard_map/all_to_all | solution.py:193
  228.0 6.0 %collective-permute-start.12 = (f32[3,2,16,128]{3,2,1,0:T(8,128)S(1)}, f32[3,2,16,128]{3,2,1,0:T(8,128)S(1)}, u32[]{:S(2)}, u32[]{:S(2)}) collective-permute-start(f32[3,2,16,128]{3,2,1,0:T(8,128)S(1)} %get-tuple-element.546), channel_id=1, source_target_pairs={{0,8},{8,16},{16,24},{24,0},{1,9},{9,17},{17,25},{25,1},{2,10},{10... | collective-permute-start | bytes 147464 | tf_op jit(solution)/shard_map/ppermute | solution.py:20
  229.2 4.8 %collective-permute-start.13 = (f32[3,2,16,128]{3,2,1,0:T(8,128)S(1)}, f32[3,2,16,128]{3,2,1,0:T(8,128)S(1)}, u32[]{:S(2)}, u32[]{:S(2)}) collective-permute-start(f32[3,2,16,128]{3,2,1,0:T(8,128)S(1)} %get-tuple-element.545), channel_id=1, source_target_pairs={{8,0},{16,8},{24,16},{0,24},{9,1},{17,9},{25,17},{1,25},{10,2},{18... | collective-permute-start | bytes 147464 | tf_op jit(solution)/shard_map/ppermute | solution.py:22
  234.2 14.1 %copy-start.4 = (s32[6]{0:T(128)S(1)}, s32[6]{0:T(128)}, u32[]{:S(2)}) copy-start(s32[6]{0:T(128)} %copy-done.3) | copy-start | bytes 76
  234.2 10.3 %collective-permute-start.14 = (f32[3,100,2,128]{3,2,1,0:T(2,128)S(1)}, f32[3,100,2,128]{3,2,1,0:T(2,128)S(1)}, u32[]{:S(2)}, u32[]{:S(2)}) collective-permute-start(f32[3,100,2,128]{3,2,1,0:T(2,128)S(1)} %get-tuple-element.542), channel_id=1, source_target_pairs={{0,1},{1,2},{2,3},{3,4},{4,5},{5,6},{6,7},{7,0},{8,9},{9,10},{10,1... | collective-permute-start | bytes 921608 | tf_op jit(solution)/shard_map/ppermute | solution.py:20
  234.3 10.3 %collective-permute-start.15 = (f32[3,100,2,128]{3,2,1,0:T(2,128)S(1)}, f32[3,100,2,128]{3,2,1,0:T(2,128)S(1)}, u32[]{:S(2)}, u32[]{:S(2)}) collective-permute-start(f32[3,100,2,128]{3,2,1,0:T(2,128)S(1)} %get-tuple-element.541), channel_id=1, source_target_pairs={{1,0},{2,1},{3,2},{4,3},{5,4},{6,5},{7,6},{0,7},{9,8},{10,9},{11,1... | collective-permute-start | bytes 921608 | tf_op jit(solution)/shard_map/ppermute | solution.py:22
  300.2 6.7 %collective-permute-start.16 = (f32[3,2,16,128]{3,2,1,0:T(8,128)S(1)}, f32[3,2,16,128]{3,2,1,0:T(8,128)S(1)}, u32[]{:S(2)}, u32[]{:S(2)}) collective-permute-start(f32[3,2,16,128]{3,2,1,0:T(8,128)S(1)} %get-tuple-element.544), channel_id=1, source_target_pairs={{0,8},{8,16},{16,24},{24,0},{1,9},{9,17},{17,25},{25,1},{2,10},{10... | collective-permute-start | bytes 147464 | tf_op jit(solution)/shard_map/ppermute | solution.py:20
  301.6 5.3 %collective-permute-start.17 = (f32[3,2,16,128]{3,2,1,0:T(8,128)S(1)}, f32[3,2,16,128]{3,2,1,0:T(8,128)S(1)}, u32[]{:S(2)}, u32[]{:S(2)}) collective-permute-start(f32[3,2,16,128]{3,2,1,0:T(8,128)S(1)} %get-tuple-element.543), channel_id=1, source_target_pairs={{8,0},{16,8},{24,16},{0,24},{9,1},{17,9},{25,17},{1,25},{10,2},{18... | collective-permute-start | bytes 147464 | tf_op jit(solution)/shard_map/ppermute | solution.py:22
  307.1 10.0 %collective-permute-start.18 = (f32[3,100,2,128]{3,2,1,0:T(2,128)S(1)}, f32[3,100,2,128]{3,2,1,0:T(2,128)S(1)}, u32[]{:S(2)}, u32[]{:S(2)}) collective-permute-start(f32[3,100,2,128]{3,2,1,0:T(2,128)S(1)} %get-tuple-element.540), channel_id=1, source_target_pairs={{0,1},{1,2},{2,3},{3,4},{4,5},{5,6},{6,7},{7,0},{8,9},{9,10},{10,1... | collective-permute-start | bytes 921608 | tf_op jit(solution)/shard_map/ppermute | solution.py:20
  307.2 10.0 %collective-permute-start.19 = (f32[3,100,2,128]{3,2,1,0:T(2,128)S(1)}, f32[3,100,2,128]{3,2,1,0:T(2,128)S(1)}, u32[]{:S(2)}, u32[]{:S(2)}) collective-permute-start(f32[3,100,2,128]{3,2,1,0:T(2,128)S(1)} %get-tuple-element.539), channel_id=1, source_target_pairs={{1,0},{2,1},{3,2},{4,3},{5,4},{6,5},{7,6},{0,7},{9,8},{10,9},{11,1... | collective-permute-start | bytes 921608 | tf_op jit(solution)/shard_map/ppermute | solution.py:22
where the time goes:
time: 332 us; the launch traced here: 325 us
  waiting for transfers between devices  84.7 us (26%)
  matrix products  64.6 us (19%)
  blocking collectives  58.7 us (18%)
  starting transfers between devices  47.3 us (14%)
  local copies, waits for them, and re-layouts  40.7 us (12%)
  other arithmetic  28 us (8%)
    all_to_all x1, blocking collectives, body(): lax.all_to_all(supplied.reshape(peer_count, CAP, BX, BY, depth_cells), 'g...  29.7 us
    ppermute x10, waiting for transfers between devices, with_halo(): lax.ppermute(tail, axis, [(i, (i + 1) % count) for i in range(count)])  29.2 us
    ppermute x10, starting transfers between devices, with_halo(): lax.ppermute(head, axis, [((i + 1) % count, i) for i in range(count)])  29.1 us
    all_to_all x1, blocking collectives, body(): lax.all_to_all(outbox, 'gy', split_axis=0, concat_axis=0, tiled=True)  29 us
    all_to_all x1, waiting for transfers between devices, body(): lax.all_to_all(supplied.reshape(peer_count, CAP, BX, BY, depth_cells), 'g...  26.6 us
    all_to_all x1, waiting for transfers between devices, body(): lax.all_to_all(outbox, 'gy', split_axis=0, concat_axis=0, tiled=True)  24.5 us
    dot_general x2, matrix products, interpolate(): jnp.einsum('nabz,ncz->nabc', windows, weight_depth, precision=high)  17.6 us
    dot_general x2, matrix products, interpolate_adjoint(): jnp.einsum('ncz,nabc->nabz', weight_depth, along_rows, precision=high)  17.5 us
  transfers between devices with their start and end apart: 23, of which 12 were waited for; matrix products, arithmetic and copies ran while one was open for 7% of the time, Pallas kernels for 0%

commit v1 on v0

v1 whole, which is shorter than its diff:
```python
import functools

import jax
import jax.numpy as jnp
from jax import lax
from jax.experimental import pallas as pl
from jax.experimental.pallas import tpu as pltpu
from jax.sharding import PartitionSpec as P

BX = 16
BY = 16
CAP = 2
QF = 8
STEPS = 2
STEP_SIZE = 1.0 / STEPS
WIN = BX + 3
LANES = 24
VMEM_LIMIT = 40 * 1024 * 1024
F32 = jnp.float32


def shape(*dims):
    return jax.ShapeDtypeStruct(dims, F32)


def exchange(name, collective_id, operands, out_shapes, plan):
    n_gx, n_gy = lax.axis_size("gx"), lax.axis_size("gy")
    count = len(operands)

    def kernel(*refs):
        ins = refs[:count]
        outs = refs[count : count + len(out_shapes)]
        send_sem, recv_sem, local_sem = refs[count + len(out_shapes) :]
        gx, gy = lax.axis_index("gx"), lax.axis_index("gy")

        def device(step_x, step_y):
            return (lax.rem(gx + step_x + n_gx, n_gx), lax.rem(gy + step_y + n_gy, n_gy))

        remote, local, peers = plan(ins, outs, gy, n_gy)
        barrier = pltpu.get_barrier_semaphore()
        for peer in peers:
            pl.semaphore_signal(
                barrier, inc=1, device_id=device(*peer), device_id_type=pl.DeviceIdType.MESH
            )
        own = [
            pltpu.make_async_copy(src, dst, local_sem.at[i]) for i, (src, dst) in enumerate(local)
        ]
        for copy in own:
            copy.start()
        pl.semaphore_wait(barrier, len(peers))
        copies = []
        for i, (src, dst, step_x, step_y) in enumerate(remote):
            copy = pltpu.make_async_remote_copy(
                src_ref=src,
                dst_ref=dst,
                send_sem=send_sem.at[i],
                recv_sem=recv_sem.at[i],
                device_id=device(step_x, step_y),
                device_id_type=pl.DeviceIdType.MESH,
            )
            copy.start()
            copies.append(copy)
        for copy in own:
            copy.wait()
        for copy in copies:
            copy.wait()

    slots = 3 * n_gy + 8
    return pl.pallas_call(
        kernel,
        name=name,
        out_shape=out_shapes,
        in_specs=[pl.BlockSpec(memory_space=pl.ANY)] * count,
        out_specs=[pl.BlockSpec(memory_space=pl.ANY)] * len(out_shapes),
        scratch_shapes=[
            pltpu.SemaphoreType.DMA((slots,)),
            pltpu.SemaphoreType.DMA((slots,)),
            pltpu.SemaphoreType.DMA((2,)),
        ],
        compiler_params=pltpu.CompilerParams(
            collective_id=collective_id, has_side_effects=True, vmem_limit_bytes=VMEM_LIMIT
        ),
    )(*operands)


NEIGHBOURS = [(i, j) for i in (-1, 0, 1) for j in (-1, 0, 1) if (i, j) != (0, 0)]


def states_plan(ins, outs, gy, n_gy):
    rows, cols, request = ins
    rows_in, cols_in, requested = outs
    remote = [
        (rows.at[0], rows_in.at[0], 1, 0),
        (rows.at[1], rows_in.at[1], -1, 0),
        (cols.at[0], cols_in.at[0], 0, 1),
        (cols.at[1], cols_in.at[1], 0, -1),
    ]
    for step in range(1, n_gy):
        peer = lax.rem(gy + step, n_gy)
        remote.append((request.at[peer], requested.at[gy], 0, step))
    local = [(request.at[gy], requested.at[gy])]
    return remote, local, [(1, 0), (-1, 0)] + [(0, step) for step in range(1, n_gy)]


def halo_plan(ins, outs, gy, n_gy):
    field, cols = ins
    rows_in, cols_in = outs
    rows = field.shape[0]
    main, low, high = pl.ds(8, rows), pl.ds(0, 8), pl.ds(rows + 8, 8)
    first, last = pl.ds(0, 8), pl.ds(rows - 8, 8)
    one, two = pl.ds(0, 1), pl.ds(1, 2)
    remote = [
        (cols.at[one], cols_in.at[one, main], 0, 1),
        (cols.at[two], cols_in.at[two, main], 0, -1),
        (field.at[pl.ds(rows - 1, 1)], rows_in.at[one], 1, 0),
        (field.at[pl.ds(0, 2)], rows_in.at[two], -1, 0),
        (cols.at[one, last], cols_in.at[one, low], 1, 1),
        (cols.at[one, first], cols_in.at[one, high], -1, 1),
        (cols.at[two, last], cols_in.at[two, low], 1, -1),
        (cols.at[two, first], cols_in.at[two, high], -1, -1),
    ]
    return remote, [], NEIGHBOURS


def fold_plan(ins, outs, gy, n_gy):
    rows_out, cols = ins
    rows_in, cols_in = outs
    rows = cols.shape[1] - 16
    main, low, high = pl.ds(8, rows), pl.ds(0, 8), pl.ds(rows + 8, 8)
    one, two = pl.ds(0, 1), pl.ds(1, 2)
    remote = [
        (cols.at[one, main], cols_in.at[one, main], 0, -1),
        (cols.at[two, main], cols_in.at[two, main], 0, 1),
        (rows_out.at[one], rows_in.at[one], -1, 0),
        (rows_out.at[two], rows_in.at[two], 1, 0),
        (cols.at[one, low], cols_in.at[one, high], -1, -1),
        (cols.at[one, high], cols_in.at[one, low], 1, -1),
        (cols.at[two, low], cols_in.at[two, high], -1, 1),
        (cols.at[two, high], cols_in.at[two, low], 1, 1),
    ]
    return remote, [], NEIGHBOURS


def bricks_plan(ins, outs, gy, n_gy):
    (outbox,), (inbox,) = ins, outs
    mine = pl.ds(gy * CAP, CAP)
    remote = []
    for step in range(1, n_gy):
        peer = lax.rem(gy + step, n_gy)
        remote.append((outbox.at[pl.ds(peer * CAP, CAP)], inbox.at[mine], 0, step))
    return remote, [(outbox.at[mine], inbox.at[mine])], [(0, step) for step in range(1, n_gy)]


def cubic_weights(f):
    return (
        -f * (f - 1.0) * (f - 2.0) * (1.0 / 6.0),
        (f + 1.0) * (f - 1.0) * (f - 2.0) * 0.5,
        -(f + 1.0) * f * (f - 2.0) * 0.5,
        (f + 1.0) * f * (f - 1.0) * (1.0 / 6.0),
    )


def slot_weights(codes, slot):
    u, v, q = codes[3 * slot], codes[3 * slot + 1], codes[3 * slot + 2]
    depth_shift = lax.shift_right_logical(q, 3)
    fractions = [u, v, jnp.bitwise_and(q, QF - 1)]
    return depth_shift, [cubic_weights(f.astype(F32) * (1.0 / QF)) for f in fractions]


def weighted(weights, terms):
    total = weights[0] * terms[0]
    for weight, term in zip(weights[1:], terms[1:]):
        total = total + weight * term
    return total


def pull_brick(window, shift, weights):
    depth = window.shape[2]
    rows = weighted(weights[0], [window[r : r + BX] for r in range(4)])
    cols = weighted(
        weights[1],
        [(rows if t == 0 else pltpu.roll(rows, LANES - t, 1))[:, :BY] for t in range(4)],
    )
    base = pltpu.roll(cols, lax.rem(depth + 1 - shift, depth), 2)
    return weighted(
        weights[2], [base if m == 0 else pltpu.roll(base, depth - m, 2) for m in range(4)]
    )


def push_brick(values, shift, weights):
    depth = values.shape[2]
    base = pltpu.roll(values, lax.rem(depth - 1 + shift, depth), 2)
    along = weighted(weights[2], [base if m == 0 else pltpu.roll(base, m, 2) for m in range(4)])
    wide = jnp.concatenate([along, jnp.zeros((BX, LANES - BY, depth), F32)], axis=1)
    cols = weighted(weights[1], [wide if t == 0 else pltpu.roll(wide, t, 1) for t in range(4)])
    parts = []
    for r in range(4):
        pieces = [cols * weights[0][r]]
        if r > 0:
            pieces.insert(0, jnp.zeros((r, LANES, depth), F32))
        if r < 3:
            pieces.append(jnp.zeros((3 - r, LANES, depth), F32))
        parts.append(jnp.concatenate(pieces, axis=0))
    return parts[0] + parts[1] + parts[2] + parts[3]


def assemble(extended, field, rows_in, cols_in):
    rows = field.shape[0]
    extended[1 : rows + 1, 1 : BY + 1, :] = field[...]
    extended[0:1, 1 : BY + 1, :] = rows_in[0:1]
    extended[rows + 1 : rows + 3, 1 : BY + 1, :] = rows_in[1:3]
    for col, side in ((0, 0), (BY + 1, 1), (BY + 2, 2)):
        extended[:, col, :] = cols_in[side, 7 : rows + 10, :]


def emit_margins(total, acc, rows_out, cols_out):
    rows = total.shape[0]
    total[...] = acc[1 : rows + 1, 1 : BY + 1, :]
    rows_out[0:1] = acc[0:1, 1 : BY + 1, :]
    rows_out[1:3] = acc[rows + 1 : rows + 3, 1 : BY + 1, :]
    cols_out[...] = jnp.zeros_like(cols_out)
    for col, side in ((0, 0), (BY + 1, 1), (BY + 2, 2)):
        cols_out[side, 7 : rows + 10, :] = acc[:, col, :]


def pull_kernel(owners, codes, field, rows_in, cols_in, out, extended):
    slot = pl.program_id(0)

    @pl.when(slot == 0)
    def _():
        assemble(extended, field, rows_in, cols_in)

    owner = owners[slot]

    @pl.when(owner >= 0)
    def _():
        shift, weights = slot_weights(codes, slot)
        out[0] = pull_brick(extended[pl.ds(owner * BX, WIN)], shift, weights)


def pull_push_kernel(
    owners, codes, field, rows_in, cols_in, total, rows_out, cols_out, extended, acc
):
    slot = pl.program_id(0)

    @pl.when(slot == 0)
    def _():
        assemble(extended, field, rows_in, cols_in)
        acc[...] = jnp.zeros_like(acc)

    owner = owners[slot]

    @pl.when(owner >= 0)
    def _():
        shift, weights = slot_weights(codes, slot)
        window = pl.ds(owner * BX, WIN)
        brick = pull_brick(extended[window], shift, weights)
        acc[window] = acc[window] + push_brick(brick, shift, weights)

    @pl.when(slot == pl.num_programs(0) - 1)
    def _():
        emit_margins(total, acc, rows_out, cols_out)


def push_kernel(owners, codes, inbox, total, rows_out, cols_out, acc):
    slot = pl.program_id(0)

    @pl.when(slot == 0)
    def _():
        acc[...] = jnp.zeros_like(acc)

    owner = owners[slot]

    @pl.when(owner >= 0)
    def _():
        shift, weights = slot_weights(codes, slot)
        window = pl.ds(owner * BX, WIN)
        acc[window] = acc[window] + push_brick(inbox[0], shift, weights)

    @pl.when(slot == pl.num_programs(0) - 1)
    def _():
        emit_margins(total, acc, rows_out, cols_out)


def gradient(states, rows_in, cols_in, step, block, blocks):
    rows, depth = states.shape[1], states.shape[3]
    first = block * BX
    cells = states[step, pl.ds(first, BX)]
    before = states[step, pl.ds(jnp.maximum(first - 1, 0), 1)]
    after = states[step, pl.ds(jnp.minimum(first + BX, rows - 1), 1)]
    before = jnp.where(block == 0, rows_in[0, pl.ds(step, 1)], before)
    after = jnp.where(block == blocks - 1, rows_in[1, pl.ds(step, 1)], after)
    left = cols_in[0, step, pl.ds(first, BX)][:, None, :]
    right = cols_in[1, step, pl.ds(first, BX)][:, None, :]
    col = lax.broadcasted_iota(jnp.int32, cells.shape, 1)
    below = jnp.concatenate([before, cells[:-1]], axis=0)
    above = jnp.concatenate([cells[1:], after], axis=0)
    lower = jnp.where(col == 0, left, pltpu.roll(cells, 1, 1))
    upper = jnp.where(col == BY - 1, right, pltpu.roll(cells, BY - 1, 1))
    return (
        (above - below) * 0.5,
        (upper - lower) * 0.5,
        (pltpu.roll(cells, depth - 1, 2) - pltpu.roll(cells, 1, 2)) * 0.5,
    )


def emit_field(values, field, cols):
    field[...] = values
    for side, col in ((0, BY - 1), (1, 0), (2, 1)):
        cols[side] = values[:, col, :]


def source_kernel(states, rows_in, cols_in, velocity, field, cols, later):
    block, blocks = pl.program_id(0), pl.num_programs(0)
    terms = []
    for step in range(STEPS):
        parts = gradient(states, rows_in, cols_in, step, block, blocks)
        terms.append(
            (velocity[0] * parts[0] + velocity[1] * parts[1] + velocity[2] * parts[2]) * -STEP_SIZE
        )
    emit_field(terms[0], field, cols)
    later[...] = terms[1]


def tangent_kernel(pulls, inbox, later, field, cols):
    emit_field(inbox[0] + later[...], field, cols)


def fold(total, rows_in, cols_in):
    block, blocks = pl.program_id(0), pl.num_programs(0)
    depth = total.shape[2]
    is_first, is_last = block == 0, block == blocks - 1
    rows = cols_in.shape[1] - 16
    zeros = jnp.zeros((8, depth), F32)
    values = total[...]
    col = lax.broadcasted_iota(jnp.int32, values.shape, 1)
    row = lax.broadcasted_iota(jnp.int32, values.shape, 0)
    values = values + jnp.where(jnp.logical_and(is_last, row == BX - 1), rows_in[0:1], 0.0)
    for i in range(2):
        values = values + jnp.where(
            jnp.logical_and(is_first, row == i), rows_in[1 + i : 2 + i], 0.0
        )
    for side, place in ((0, BY - 1), (1, 0), (2, 1)):
        strip = cols_in[side, pl.ds(8 + block * BX, BX)]
        low = jnp.concatenate([cols_in[side, 0:8], zeros], axis=0)
        high = jnp.concatenate([zeros, cols_in[side, rows + 8 : rows + 16]], axis=0)
        strip = strip + jnp.where(is_first, low, 0.0) + jnp.where(is_last, high, 0.0)
        values = values + jnp.where(col == place, strip[:, None, :], 0.0)
    return values


def outbox_kernel(pulls, total, rows_in, cols_in, adjoint, outbox):
    values = fold(total, rows_in, cols_in)
    adjoint[...] = values
    outbox[0] = values


def force_kernel(
    states, rows_in, cols_in, later_adjoint, total, fold_rows, fold_cols, force
):
    block, blocks = pl.program_id(0), pl.num_programs(0)
    adjoints = [fold(total, fold_rows, fold_cols), later_adjoint[...]]
    scaled = [adjoint * -STEP_SIZE for adjoint in adjoints]
    early = gradient(states, rows_in, cols_in, 0, block, blocks)
    late = gradient(states, rows_in, cols_in, 1, block, blocks)
    for c in range(3):
        force[c] = scaled[1] * late[c] + scaled[0] * early[c]


def whole(dims):
    return pl.BlockSpec(dims, lambda *_: (0,) * len(dims))


def local_call(kernel, name, steps, scalars, in_specs, out_specs, out_shapes, scratch, operands):
    return pl.pallas_call(
        kernel,
        name=name,
        grid_spec=pltpu.PrefetchScalarGridSpec(
            num_scalar_prefetch=len(scalars),
            grid=(steps,),
            in_specs=in_specs,
            out_specs=out_specs,
            scratch_shapes=scratch,
        ),
        out_shape=out_shapes,
        compiler_params=pltpu.CompilerParams(vmem_limit_bytes=VMEM_LIMIT),
    )(*scalars, *operands)


def body(velocity, states, pull_plan, send_plan, codes):
    _, rows, cols, depth = velocity.shape
    assert cols == BY and rows % BX == 0
    bricks = rows // BX
    peers = lax.axis_size("gy")
    slots = peers * CAP
    pulls = pull_plan.reshape(bricks)
    owners = send_plan.reshape(slots)
    code_flat = codes.reshape(3, bricks)

    match = pulls[None, :] == jnp.arange(slots, dtype=jnp.int32)[:, None]
    request = jnp.sum(jnp.where(match[:, None, :], code_flat[None], 0), axis=2)
    request = jnp.pad(request.reshape(peers, CAP, 3), ((0, 0), (0, 8 - CAP), (0, 125)))
    edge_rows = jnp.stack([states[:, rows - 1], states[:, 0]])
    edge_cols = jnp.stack([states[:, :, cols - 1], states[:, :, 0]])
    state_rows, state_cols, requested = exchange(
        "exchange_states",
        0,
        (edge_rows, edge_cols, request),
        [
            shape(2, STEPS, cols, depth),
            shape(2, STEPS, rows, depth),
            jax.ShapeDtypeStruct((peers, 8, 128), jnp.int32),
        ],
        states_plan,
    )
    slot_codes = requested[:, :CAP, :3].reshape(slots * 3)

    block = pl.BlockSpec((BX, BY, depth), lambda k, *_: (k, 0, 0))
    vector_block = pl.BlockSpec((3, BX, BY, depth), lambda k, *_: (0, k, 0, 0))
    edge_block = pl.BlockSpec((3, BX, depth), lambda k, *_: (0, k, 0))
    slot_block = pl.BlockSpec((1, BX, BY, depth), lambda s, *_: (s, 0, 0, 0))
    named_block = pl.BlockSpec((1, BX, BY, depth), lambda k, plan: (plan[k], 0, 0, 0))
    state_specs = [whole(states.shape), whole(state_rows.shape), whole(state_cols.shape)]
    field_shape = shape(rows, cols, depth)
    edge_shape = shape(3, rows, depth)
    margin_shapes = [shape(3, cols, depth), shape(3, rows + 16, depth)]
    margin_specs = [whole(s.shape) for s in margin_shapes]
    field_spec = whole(field_shape.shape)
    slot_shape = shape(slots, BX, BY, depth)
    extended = pltpu.VMEM((rows + 3, LANES, depth), F32)

    field, edges, later = local_call(
        source_kernel, "source", bricks, (), state_specs + [vector_block],
        [block, edge_block, block], [field_shape, edge_shape, field_shape], [],
        (states, state_rows, state_cols, velocity),
    )
    halo = exchange("exchange_source", 1, (field, edges), margin_shapes, halo_plan)
    supplied = local_call(
        pull_kernel, "pull", slots, (owners, slot_codes), [field_spec] + margin_specs,
        slot_block, slot_shape, [extended], (field, *halo),
    )
    (inbox,) = exchange("exchange_pulled", 2, (supplied,), [slot_shape], bricks_plan)
    field, edges = local_call(
        tangent_kernel, "tangent", bricks, (pulls,), [named_block, block],
        [block, edge_block], [field_shape, edge_shape], [], (inbox, later),
    )
    halo = exchange("exchange_tangent", 3, (field, edges), margin_shapes, halo_plan)
    total, *margins = local_call(
        pull_push_kernel, "pull_push", slots, (owners, slot_codes), [field_spec] + margin_specs,
        [field_spec] + margin_specs, [field_shape] + margin_shapes, [extended, extended],
        (field, *halo),
    )
    margins = exchange("fold_late", 4, margins, margin_shapes, fold_plan)
    late_adjoint, outbox = local_call(
        outbox_kernel, "outbox", bricks, (pulls,), [block] + margin_specs,
        [block, named_block], [field_shape, slot_shape], [], (total, *margins),
    )
    (inbox,) = exchange("exchange_adjoint", 5, (outbox,), [slot_shape], bricks_plan)
    total, *margins = local_call(
        push_kernel, "push", slots, (owners, slot_codes), [slot_block],
        [field_spec] + margin_specs, [field_shape] + margin_shapes, [extended], (inbox,),
    )
    margins = exchange("fold_early", 6, margins, margin_shapes, fold_plan)
    return local_call(
        force_kernel, "force", bricks, (), state_specs + [block, block] + margin_specs,
        vector_block, shape(3, rows, cols, depth), [],
        (states, state_rows, state_cols, late_adjoint, total, *margins),
    )


def solution(mesh):
    return jax.shard_map(
        body,
        mesh=mesh,
        in_specs=(
            P(None, "gx", "gy", None),
            P(None, "gx", "gy", None),
            P("gx", "gy"),
            P("gx", "gy", None, None),
            P(None, "gx", "gy"),
        ),
        out_specs=P(None, "gx", "gy", None),
        check_vma=False,
    )
```

time: 332 us -> 129 us (0.39); the launches traced: 325 us -> 131 us
  Pallas kernels: 0 us -> 123 us
  waiting for transfers between devices: 84.7 us -> 0 us
  matrix products: 64.6 us -> 0 us
  blocking collectives: 58.7 us -> 0 us
  starting transfers between devices: 47.3 us -> 0 us
  local copies, waits for them, and re-layouts: 40.7 us -> 7.03 us
  other arithmetic: 28 us -> 0.84 us
    pallas_call x0 -> x14, Pallas kernels: none -> 123 us  [the longest x7 97.3 us: exchange(): pl.pallas_call(kernel, name=name, out_shape=out_shapes, in_specs=[pl.Bloc...]
    dot_general x14 -> x0, matrix products: 64.6 us -> none  [the longest x2 17.6 us: interpolate(): jnp.einsum('nabz,ncz->nabc', windows, weight_depth, precision=high)]
    all_to_all x2 -> x0, blocking collectives: 58.7 us -> none  [the longest x1 29.7 us: body(): lax.all_to_all(supplied.reshape(peer_count, CAP, BX, BY, depth_cells), 'g...]
    all_to_all x3 -> x0, waiting for transfers between devices: 51.1 us -> none  [the longest x1 26.6 us: body(): lax.all_to_all(supplied.reshape(peer_count, CAP, BX, BY, depth_cells), 'g...]
    ppermute x20 -> x0, starting transfers between devices: 35.1 us -> none  [the longest x10 29.1 us: with_halo(): lax.ppermute(head, axis, [((i + 1) % count, i) for i in range(count)])]
    ppermute x20 -> x0, waiting for transfers between devices: 33.6 us -> none  [the longest x10 29.2 us: with_halo(): lax.ppermute(tail, axis, [(i, (i + 1) % count) for i in range(count)])]
    all_to_all x3 -> x0, starting transfers between devices: 12.2 us -> none  [the longest x1 4.2 us: body(): lax.all_to_all(outbox, 'gy', split_axis=0, concat_axis=0, tiled=True)]
    gather x4 -> x0, local copies, waits for them, and re-layouts: 7.44 us -> none  [the longest x2 5.36 us: body(): jnp.take(windows, send_flat, axis=0)]
  transfers between devices with their start and end apart: 23 -> 0, of which waited for: 12 -> 0; matrix products, arithmetic and copies ran while one was open for 7% -> 0% of each run, Pallas kernels for 0% -> 0%
where the time goes in v1:
time: 129 us; the launch traced here: 131 us
  Pallas kernels  123 us (95%)
  local copies, waits for them, and re-layouts  7.03 us (5%)
    pallas_call x7, Pallas kernels, exchange(): pl.pallas_call(kernel, name=name, out_shape=out_shapes, in_specs=[pl.Bloc...  97.3 us
    pallas_call x7, Pallas kernels, local_call(): pl.pallas_call(kernel, name=name, grid_spec=pltpu.PrefetchScalarGridSpec(...  25.7 us
    unnamed x10, local copies, waits for them, and re-layouts  4.52 us

profile of v1, /device:TPU:0, one launch (start us, length us, event | category | flops | bytes accessed | tf_op | source)
XLA Modules:
  0.0 131.0 jit_solution(6582536825658079391)
XLA Ops:
  0.0 0.7 iota_compare_fusion
  0.7 0.7 copy.31
  1.4 0.1 select_reduce_fusion
  1.5 0.8 copy.23
  2.3 0.1 reshape.32.owners
  2.3 0.1 copy.24
  2.4 0.7 slice_bitcast_fusion.1
  3.2 1.5 %fusion = (f32[2,96,1,128]{3,2,1,0:T(1,128)S(1)}, f32[2,96,1,128]{3,2,1,0:T(1,128)S(1)}) fusion(f32[2,96,16,128]{3,2,1,0:T(8,128)} %states.3), kind=kLoop, calls=%fused_computation.7 | loop fusion | bytes 393216 | tf_op jit(solution)/shard_map/slice | solution.py:404
  4.7 10.9 %exchange_states.1 = (f32[2,2,16,128]{3,2,1,0:T(8,128)S(1)}, f32[2,2,96,128]{3,2,1,0:T(8,128)S(1)}, s32[8,8,128]{2,1,0:T(8,128)S(1)}) custom-call(f32[2,2,16,128]{3,2,1,0:T(8,128)S(1)} %pad_maximum_fusion.1.refs_0_, f32[2,2,96,128]{3,2,1,0:T(8,128)S(1)} %pad_maximum_fusion.refs_1_, s32[8,8,128]{2,1,0:T(8,128)S(1)} %pad.4.refs_2_), custom_call_target="tpu_custom_call" | custom-call | tf_op jit(solution)/shard_map/exchange_states/pallas_call | solution.py:69
  15.6 0.1 reshape.33.codes
  15.7 0.0 copy-start
  15.7 1.4 %copy-done = f32[2,96,16,128]{3,2,1,0:T(8,128)S(1)} copy-done((f32[2,96,16,128]{3,2,1,0:T(8,128)S(1)}, f32[2,96,16,128]{3,2,1,0:T(8,128)}, u32[]{:S(2)}) %copy-start) | copy-done | bytes 1572888
  17.1 0.0 copy-start.2
  17.1 1.7 %copy-done.2 = f32[3,96,16,128]{3,2,1,0:T(8,128)S(1)} copy-done((f32[3,96,16,128]{3,2,1,0:T(8,128)S(1)}, f32[3,96,16,128]{3,2,1,0:T(8,128)}, u32[]{:S(2)}) %copy-start.2) | copy-done | bytes 2359320
  18.8 1.6 %source.1 = (f32[96,16,128]{2,1,0:T(8,128)S(1)}, f32[3,96,128]{2,1,0:T(8,128)S(1)}, f32[96,16,128]{2,1,0:T(8,128)S(1)}) custom-call(f32[2,96,16,128]{3,2,1,0:T(8,128)S(1)} %copy-done, f32[2,2,16,128]{3,2,1,0:T(8,128)S(1)} %get-tuple-element.29.rows_in, f32[2,2,96,128]{3,2,1,0:T(8,128)S(1)} %get-tuple-element.30.cols_in, f32[3,96,16,128]{3,2,1,0:T(8,128)S(1)} %copy-done.2), custom_call_target="tpu_custom_call" | custom-call | tf_op jit(solution)/shard_map/source/pallas_call | solution.py:375
  20.4 7.5 %exchange_source.1 = (f32[3,16,128]{2,1,0:T(8,128)S(1)}, f32[3,112,128]{2,1,0:T(8,128)S(1)}) custom-call(f32[96,16,128]{2,1,0:T(8,128)S(1)} %get-tuple-element.32.refs_0_.field, f32[3,96,128]{2,1,0:T(8,128)S(1)} %get-tuple-element.33.refs_1_), custom_call_target="tpu_custom_call" | custom-call | tf_op jit(solution)/shard_map/exchange_source/pallas_call | solution.py:69
  27.9 4.9 %pull.1.refs_0_ = f32[16,16,16,128]{3,2,1,0:T(8,128)S(1)} custom-call(s32[16]{0:T(128)S(1)} %reshape.32.owners, s32[48]{0:T(128)S(1)} %reshape.33.codes, f32[96,16,128]{2,1,0:T(8,128)S(1)} %get-tuple-element.32.refs_0_.field, f32[3,16,128]{2,1,0:T(8,128)S(1)} %get-tuple-element.34.rows_in, f32[3,112,128]{2,1,0:T(8,128)S(1)} %get-tuple-element.35.cols_in), custom_call_target="tpu_custom_call" | custom-call | tf_op jit(solution)/shard_map/pull/pallas_call | solution.py:375
  32.8 0.0 copy-start.3
  32.8 24.3 %exchange_pulled.1.inbox = f32[16,16,16,128]{3,2,1,0:T(8,128)S(1)} custom-call(f32[16,16,16,128]{3,2,1,0:T(8,128)S(1)} %pull.1.refs_0_), custom_call_target="tpu_custom_call" | custom-call | tf_op jit(solution)/shard_map/exchange_pulled/pallas_call | solution.py:69
  57.1 0.0 copy-done.3
  57.1 0.8 tangent.1
  57.9 9.0 %exchange_tangent.1 = (f32[3,16,128]{2,1,0:T(8,128)S(1)}, f32[3,112,128]{2,1,0:T(8,128)S(1)}) custom-call(f32[96,16,128]{2,1,0:T(8,128)S(1)} %get-tuple-element.37.refs_0_.field, f32[3,96,128]{2,1,0:T(8,128)S(1)} %get-tuple-element.38.refs_1_), custom_call_target="tpu_custom_call" | custom-call | tf_op jit(solution)/shard_map/exchange_tangent/pallas_call | solution.py:69
  67.0 8.9 %pull_push.1 = (f32[96,16,128]{2,1,0:T(8,128)S(1)}, f32[3,16,128]{2,1,0:T(8,128)S(1)}, f32[3,112,128]{2,1,0:T(8,128)S(1)}) custom-call(s32[16]{0:T(128)S(1)} %reshape.32.owners, s32[48]{0:T(128)S(1)} %reshape.33.codes, f32[96,16,128]{2,1,0:T(8,128)S(1)} %get-tuple-element.37.refs_0_.field, f32[3,16,128]{2,1,0:T(8,128)S(1)} %get-tuple-element.39.rows_in, ...), custom_call_target="tpu_custom_call" | custom-call | tf_op jit(solution)/shard_map/pull_push/pallas_call | solution.py:375
  75.8 10.6 %fold_late.1 = (f32[3,16,128]{2,1,0:T(8,128)S(1)}, f32[3,112,128]{2,1,0:T(8,128)S(1)}) custom-call(f32[3,16,128]{2,1,0:T(8,128)S(1)} %get-tuple-element.42.refs_0_, f32[3,112,128]{2,1,0:T(8,128)S(1)} %get-tuple-element.43.refs_1_), custom_call_target="tpu_custom_call" | custom-call | tf_op jit(solution)/shard_map/fold_late/pallas_call | solution.py:69
  86.5 0.9 outbox.1
  87.4 24.8 %exchange_adjoint.1.inbox = f32[16,16,16,128]{3,2,1,0:T(8,128)S(1)} custom-call(f32[16,16,16,128]{3,2,1,0:T(8,128)S(1)} %get-tuple-element.47.refs_0_), custom_call_target="tpu_custom_call" | custom-call | tf_op jit(solution)/shard_map/exchange_adjoint/pallas_call | solution.py:69
  112.2 0.0 copy-start.1
  112.2 5.3 %push.1 = (f32[96,16,128]{2,1,0:T(8,128)S(1)}, f32[3,16,128]{2,1,0:T(8,128)S(1)}, f32[3,112,128]{2,1,0:T(8,128)S(1)}) custom-call(s32[16]{0:T(128)S(1)} %reshape.32.owners, s32[48]{0:T(128)S(1)} %reshape.33.codes, f32[16,16,16,128]{3,2,1,0:T(8,128)S(1)} %exchange_adjoint.1.inbox), custom_call_target="tpu_custom_call" | custom-call | tf_op jit(solution)/shard_map/push/pallas_call | solution.py:375
  117.5 10.2 %fold_early.1 = (f32[3,16,128]{2,1,0:T(8,128)S(1)}, f32[3,112,128]{2,1,0:T(8,128)S(1)}) custom-call(f32[3,16,128]{2,1,0:T(8,128)S(1)} %get-tuple-element.49.refs_0_, f32[3,112,128]{2,1,0:T(8,128)S(1)} %get-tuple-element.50.refs_1_), custom_call_target="tpu_custom_call" | custom-call | tf_op jit(solution)/shard_map/fold_early/pallas_call | solution.py:69
  127.7 0.0 copy-done.1
  127.7 3.3 %force.1 = f32[3,96,16,128]{3,2,1,0:T(8,128)} custom-call(f32[2,96,16,128]{3,2,1,0:T(8,128)S(1)} %copy-done.1, f32[2,2,16,128]{3,2,1,0:T(8,128)S(1)} %get-tuple-element.29.rows_in, f32[2,2,96,128]{3,2,1,0:T(8,128)S(1)} %get-tuple-element.30.cols_in, f32[96,16,128]{2,1,0:T(8,128)S(1)} %get-tuple-element.46.later_adjoint, ...), custom_call_target="tpu_custom_call" | custom-call | tf_op jit(solution)/shard_map/force/pallas_call | solution.py:375
  (4 shorter events, 0.0 us)
Async XLA Ops:
  15.7 1.4 %copy-start = (f32[2,96,16,128]{3,2,1,0:T(8,128)S(1)}, f32[2,96,16,128]{3,2,1,0:T(8,128)}, u32[]{:S(2)}) copy-start(f32[2,96,16,128]{3,2,1,0:T(8,128)} %states.3) | copy-start | bytes 4718596
  17.1 1.7 %copy-start.2 = (f32[3,96,16,128]{3,2,1,0:T(8,128)S(1)}, f32[3,96,16,128]{3,2,1,0:T(8,128)}, u32[]{:S(2)}) copy-start(f32[3,96,16,128]{3,2,1,0:T(8,128)} %velocity.1) | copy-start | bytes 7077892
  32.8 24.3 %copy-start.3 = (s32[6,1]{0,1:T(1,128)S(1)}, s32[6,1]{0,1:T(1,128)}, u32[]{:S(2)}) copy-start(s32[6,1]{0,1:T(1,128)} %param.7) | copy-start | bytes 76
  112.2 15.5 %copy-start.1 = (f32[2,96,16,128]{3,2,1,0:T(8,128)S(1)}, f32[2,96,16,128]{3,2,1,0:T(8,128)}, u32[]{:S(2)}) copy-start(f32[2,96,16,128]{3,2,1,0:T(8,128)} %states.3) | copy-start | bytes 4718596

commit v2 on v1

--- a/solution.py
+++ b/solution.py
@@ -86,22 +86,6 @@
 NEIGHBOURS = [(i, j) for i in (-1, 0, 1) for j in (-1, 0, 1) if (i, j) != (0, 0)]
 
 
-def states_plan(ins, outs, gy, n_gy):
-    rows, cols, request = ins
-    rows_in, cols_in, requested = outs
-    remote = [
-        (rows.at[0], rows_in.at[0], 1, 0),
-        (rows.at[1], rows_in.at[1], -1, 0),
-        (cols.at[0], cols_in.at[0], 0, 1),
-        (cols.at[1], cols_in.at[1], 0, -1),
-    ]
-    for step in range(1, n_gy):
-        peer = lax.rem(gy + step, n_gy)
-        remote.append((request.at[peer], requested.at[gy], 0, step))
-    local = [(request.at[gy], requested.at[gy])]
-    return remote, local, [(1, 0), (-1, 0)] + [(0, step) for step in range(1, n_gy)]
-
-
 def halo_plan(ins, outs, gy, n_gy):
     field, cols = ins
     rows_in, cols_in = outs
@@ -160,11 +144,14 @@
     )
 
 
-def slot_weights(codes, slot):
-    u, v, q = codes[3 * slot], codes[3 * slot + 1], codes[3 * slot + 2]
+def code_weights(u, v, q):
     depth_shift = lax.shift_right_logical(q, 3)
     fractions = [u, v, jnp.bitwise_and(q, QF - 1)]
     return depth_shift, [cubic_weights(f.astype(F32) * (1.0 / QF)) for f in fractions]
+
+
+def slot_weights(codes, slot):
+    return code_weights(codes[3 * slot], codes[3 * slot + 1], codes[3 * slot + 2])
 
 
 def weighted(weights, terms):
@@ -221,21 +208,6 @@
     cols_out[...] = jnp.zeros_like(cols_out)
     for col, side in ((0, 0), (BY + 1, 1), (BY + 2, 2)):
         cols_out[side, 7 : rows + 10, :] = acc[:, col, :]
-
-
-def pull_kernel(owners, codes, field, rows_in, cols_in, out, extended):
-    slot = pl.program_id(0)
-
-    @pl.when(slot == 0)
-    def _():
-        assemble(extended, field, rows_in, cols_in)
-
-    owner = owners[slot]
-
-    @pl.when(owner >= 0)
-    def _():
-        shift, weights = slot_weights(codes, slot)
-        out[0] = pull_brick(extended[pl.ds(owner * BX, WIN)], shift, weights)
 
 
 def pull_push_kernel(
@@ -310,16 +282,214 @@
         cols[side] = values[:, col, :]
 
 
-def source_kernel(states, rows_in, cols_in, velocity, field, cols, later):
-    block, blocks = pl.program_id(0), pl.num_programs(0)
-    terms = []
+def supply_kernel(
+    n_gx, n_gy, pulls, owners, codes, states, velocity,
+    inbox, later, rows_in, cols_in, requested,
+    states_v, velocity_v, rows_v, cols_v, edge_cols, request, requested_v, requested_s,
+    field, edges, halo_rows, halo_cols, extended, supplied, later_v,
+    load_sem, send_sem, recv_sem, halo_send, halo_recv, code_send, code_recv,
+    brick_send, brick_recv,
+):
+    gx, gy = lax.axis_index("gx"), lax.axis_index("gy")
+    rows, depth = states.shape[1], states.shape[3]
+    blocks = rows // BX
+
+    def device(step_x, step_y):
+        return (lax.rem(gx + step_x + n_gx, n_gx), lax.rem(gy + step_y + n_gy, n_gy))
+
+    def remote(src, dst, send, recv, step_x, step_y):
+        return pltpu.make_async_remote_copy(
+            src_ref=src, dst_ref=dst, send_sem=send, recv_sem=recv,
+            device_id=device(step_x, step_y), device_id_type=pl.DeviceIdType.MESH,
+        )
+
+    peers = [(i, j) for i in (-1, 1) for j in (-1, 0, 1)] + [(0, d) for d in range(1, n_gy)]
+    barrier = pltpu.get_barrier_semaphore()
+    for peer in peers:
+        pl.semaphore_signal(
+            barrier, inc=1, device_id=device(*peer), device_id_type=pl.DeviceIdType.MESH
+        )
+    loads = [
+        pltpu.make_async_copy(states, states_v, load_sem.at[0]),
+        pltpu.make_async_copy(velocity, velocity_v, load_sem.at[1]),
+    ]
+    for load in loads:
+        load.start()
+    peer_row = lax.broadcasted_iota(jnp.int32, request.shape, 0)
+    entry = lax.broadcasted_iota(jnp.int32, request.shape, 1)
+    lane = lax.broadcasted_iota(jnp.int32, request.shape, 2)
+    place = jnp.where(entry < CAP, peer_row * CAP + entry, -1)
+    table = jnp.zeros(request.shape, jnp.int32)
+    for k in range(blocks):
+        triple = jnp.where(
+            lane == 0, codes[0, k, 0], jnp.where(lane == 1, codes[1, k, 0], codes[2, k, 0])
+        )
+        table = jnp.where(place == pulls[k, 0], triple, table)
+    request[...] = table
+    requested_v[pl.ds(gy, 1)] = request[pl.ds(gy, 1)]
+    loads[0].wait()
     for step in range(STEPS):
-        parts = gradient(states, rows_in, cols_in, step, block, blocks)
-        terms.append(
-            (velocity[0] * parts[0] + velocity[1] * parts[1] + velocity[2] * parts[2]) * -STEP_SIZE
+        edge_cols[0, step] = states_v[step, :, BY - 1, :]
+        edge_cols[1, step] = states_v[step, :, 0, :]
+    pl.semaphore_wait(barrier, len(peers))
+
+    copies = [
+        remote(edge_cols.at[0], cols_v.at[0], send_sem.at[0], recv_sem.at[0], 0, 1),
+        remote(edge_cols.at[1], cols_v.at[1], send_sem.at[1], recv_sem.at[1], 0, -1),
+        remote(states_v.at[:, rows - 1], rows_v.at[0], send_sem.at[2], recv_sem.at[2], 1, 0),
+        remote(states_v.at[:, 0], rows_v.at[1], send_sem.at[3], recv_sem.at[3], -1, 0),
+    ]
+    for copy in copies:
+        copy.start()
+    code_copies = []
+    for d in range(1, n_gy):
+        peer = lax.rem(gy + d, n_gy)
+        code_copies.append(
+            remote(request.at[peer], requested_v.at[gy], code_send.at[d], code_recv.at[d], 0, d)
         )
-    emit_field(terms[0], field, cols)
-    later[...] = terms[1]
+    for copy in code_copies:
+        copy.start()
+    loads[1].wait()
+    for copy in copies:
+        copy.wait()
+
+    @pl.loop(0, blocks)
+    def _(block):
+        cells = pl.ds(block * BX, BX)
+        terms = []
+        for step in range(STEPS):
+            parts = gradient(states_v, rows_v, cols_v, step, block, blocks)
+            terms.append(
+                (
+                    velocity_v[0, cells] * parts[0]
+                    + velocity_v[1, cells] * parts[1]
+                    + velocity_v[2, cells] * parts[2]
+                )
+                * -STEP_SIZE
+            )
+        field[cells] = terms[0]
+        for side, col in ((0, BY - 1), (1, 0), (2, 1)):
+            edges[side, cells] = terms[0][:, col, :]
+        later_v[cells] = terms[1]
+
+    plan, _, _ = halo_plan((field, edges), (halo_rows, halo_cols), gy, n_gy)
+    copies = [
+        remote(src, dst, halo_send.at[i], halo_recv.at[i], step_x, step_y)
+        for i, (src, dst, step_x, step_y) in enumerate(plan)
+    ]
+    for copy in copies:
+        copy.start()
+    saves = [
+        pltpu.make_async_copy(later_v, later, load_sem.at[0]),
+        pltpu.make_async_copy(rows_v, rows_in, load_sem.at[1]),
+        pltpu.make_async_copy(cols_v, cols_in, load_sem.at[2]),
+    ]
+    for save in saves:
+        save.start()
+    for copy in code_copies:
+        copy.wait()
+    tables = [
+        pltpu.make_async_copy(requested_v, requested_s, load_sem.at[3]),
+        pltpu.make_async_copy(requested_v, requested, load_sem.at[4]),
+    ]
+    for copy in tables:
+        copy.start()
+    for copy in tables:
+        copy.wait()
+    for copy in copies:
+        copy.wait()
+    assemble(extended, field, halo_rows, halo_cols)
+
+    def supply(peer):
+        for e in range(CAP):
+            owner = jnp.maximum(owners[0, 0, peer, e], 0)
+            shift, weights = code_weights(
+                requested_s[peer, e, 0], requested_s[peer, e, 1], requested_s[peer, e, 2]
+            )
+            supplied[peer * CAP + e] = pull_brick(
+                extended[pl.ds(owner * BX, WIN)], shift, weights
+            )
+
+    mine = pl.ds(gy * CAP, CAP)
+
+    def brick_copy(d):
+        peer = lax.rem(gy + d, n_gy)
+        return remote(
+            supplied.at[pl.ds(peer * CAP, CAP)], inbox.at[mine],
+            brick_send.at[d], brick_recv.at[d], 0, d,
+        )
+
+    @pl.loop(1, n_gy)
+    def _(d):
+        supply(lax.rem(gy + d, n_gy))
+        brick_copy(d).start()
+
+    supply(gy)
+    own = pltpu.make_async_copy(supplied.at[mine], inbox.at[mine], load_sem.at[5])
+    own.start()
+    own.wait()
+    for save in saves:
+        save.wait()
+
+    @pl.loop(1, n_gy)
+    def _(d):
+        brick_copy(d).wait()
+
+
+def supply_call(states, velocity, pull_plan, send_plan, codes):
+    n_gx, n_gy = lax.axis_size("gx"), lax.axis_size("gy")
+    _, rows, cols, depth = states.shape
+    slots = n_gy * CAP
+    table = (n_gy, 8, 128)
+    smem = pl.BlockSpec(memory_space=pltpu.SMEM)
+    any_space = pl.BlockSpec(memory_space=pl.ANY)
+    dma = pltpu.SemaphoreType.DMA
+
+    def vmem(*dims):
+        return pltpu.VMEM(dims, F32)
+
+    return pl.pallas_call(
+        lambda *refs: supply_kernel(n_gx, n_gy, *refs),
+        name="supply",
+        in_specs=[smem, smem, smem, any_space, any_space],
+        out_specs=[any_space] * 5,
+        out_shape=[
+            shape(slots, BX, BY, depth),
+            shape(rows, cols, depth),
+            shape(2, STEPS, cols, depth),
+            shape(2, STEPS, rows, depth),
+            jax.ShapeDtypeStruct(table, jnp.int32),
+        ],
+        scratch_shapes=[
+            vmem(STEPS, rows, cols, depth),
+            vmem(3, rows, cols, depth),
+            vmem(2, STEPS, cols, depth),
+            vmem(2, STEPS, rows, depth),
+            vmem(2, STEPS, rows, depth),
+            pltpu.VMEM(table, jnp.int32),
+            pltpu.VMEM(table, jnp.int32),
+            pltpu.SMEM(table, jnp.int32),
+            vmem(rows, cols, depth),
+            vmem(3, rows, depth),
+            vmem(3, cols, depth),
+            vmem(3, rows + 16, depth),
+            vmem(rows + 3, LANES, depth),
+            vmem(slots, BX, BY, depth),
+            vmem(rows, cols, depth),
+            dma((6,)),
+            dma((4,)),
+            dma((4,)),
+            dma((8,)),
+            dma((8,)),
+            dma((n_gy,)),
+            dma((n_gy,)),
+            dma((n_gy,)),
+            dma((n_gy,)),
+        ],
+        compiler_params=pltpu.CompilerParams(
+            collective_id=0, has_side_effects=True, vmem_limit_bytes=VMEM_LIMIT
+        ),
+    )(pull_plan, send_plan, codes, states, velocity)
 
 
 def tangent_kernel(pulls, inbox, later, field, cols):
@@ -395,23 +565,8 @@
     slots = peers * CAP
     pulls = pull_plan.reshape(bricks)
     owners = send_plan.reshape(slots)
-    code_flat = codes.reshape(3, bricks)
-
-    match = pulls[None, :] == jnp.arange(slots, dtype=jnp.int32)[:, None]
-    request = jnp.sum(jnp.where(match[:, None, :], code_flat[None], 0), axis=2)
-    request = jnp.pad(request.reshape(peers, CAP, 3), ((0, 0), (0, 8 - CAP), (0, 125)))
-    edge_rows = jnp.stack([states[:, rows - 1], states[:, 0]])
-    edge_cols = jnp.stack([states[:, :, cols - 1], states[:, :, 0]])
-    state_rows, state_cols, requested = exchange(
-        "exchange_states",
-        0,
-        (edge_rows, edge_cols, request),
-        [
-            shape(2, STEPS, cols, depth),
-            shape(2, STEPS, rows, depth),
-            jax.ShapeDtypeStruct((peers, 8, 128), jnp.int32),
-        ],
-        states_plan,
+    inbox, later, state_rows, state_cols, requested = supply_call(
+        states, velocity, pull_plan, send_plan, codes
     )
     slot_codes = requested[:, :CAP, :3].reshape(slots * 3)
 
@@ -429,17 +584,6 @@
     slot_shape = shape(slots, BX, BY, depth)
     extended = pltpu.VMEM((rows + 3, LANES, depth), F32)
 
-    field, edges, later = local_call(
-        source_kernel, "source", bricks, (), state_specs + [vector_block],
-        [block, edge_block, block], [field_shape, edge_shape, field_shape], [],
-        (states, state_rows, state_cols, velocity),
-    )
-    halo = exchange("exchange_source", 1, (field, edges), margin_shapes, halo_plan)
-    supplied = local_call(
-        pull_kernel, "pull", slots, (owners, slot_codes), [field_spec] + margin_specs,
-        slot_block, slot_shape, [extended], (field, *halo),
-    )
-    (inbox,) = exchange("exchange_pulled", 2, (supplied,), [slot_shape], bricks_plan)
     field, edges = local_call(
         tangent_kernel, "tangent", bricks, (pulls,), [named_block, block],
         [block, edge_block], [field_shape, edge_shape], [], (inbox, later),

time: 129 us -> 119 us (0.922); the launches traced: 131 us -> 119 us
  Pallas kernels: 123 us -> 113 us
  local copies, waits for them, and re-layouts: 7.03 us -> 5.55 us
    pallas_call x7 -> x4, Pallas kernels: 97.3 us -> 50.8 us  [exchange(): pl.pallas_call(kernel, name=name, out_shape=out_shapes, in_specs=[pl.Bloc...]
    pallas_call x0 -> x1, Pallas kernels: none -> 41.2 us  [supply_call(): pl.pallas_call(lambda *refs: supply_kernel(n_gx, n_gy, *refs), name='supp...]
    pallas_call x7 -> x5, Pallas kernels: 25.7 us -> 21.1 us  [local_call(): pl.pallas_call(kernel, name=name, grid_spec=pltpu.PrefetchScalarGridSpec(...]
    slice x1 -> x0, local copies, waits for them, and re-layouts: 1.51 us -> none  [body(): edge_cols = jnp.stack([states[:, :, cols - 1], states[:, :, 0]])]
    unnamed x10 -> x11, local copies, waits for them, and re-layouts: 4.52 us -> 5.37 us
where the time goes in v2:
time: 119 us
  Pallas kernels  113 us (95%)
  local copies, waits for them, and re-layouts  5.55 us (5%)
    pallas_call x4, Pallas kernels, exchange(): pl.pallas_call(kernel, name=name, out_shape=out_shapes, in_specs=[pl.Bloc...  50.8 us
    pallas_call x1, Pallas kernels, supply_call(): pl.pallas_call(lambda *refs: supply_kernel(n_gx, n_gy, *refs), name='supp...  41.2 us
    pallas_call x5, Pallas kernels, local_call(): pl.pallas_call(kernel, name=name, grid_spec=pltpu.PrefetchScalarGridSpec(...  21.1 us
    unnamed x11, local copies, waits for them, and re-layouts  5.37 us

profile of v2, /device:TPU:0, one launch (start us, length us, event | category | flops | bytes accessed | tf_op | source)
XLA Modules:
  0.0 118.7 jit_solution(17581455236632170767)
XLA Ops:
  0.0 0.0 copy-start.3
  0.0 0.8 copy.11.refs_1_
  0.8 0.1 reshape.10.owners
  0.9 0.7 copy.10.refs_0_
  1.6 0.8 copy.12.refs_2_
  2.4 0.0 copy-start
  2.4 1.4 %copy-done = f32[2,96,16,128]{3,2,1,0:T(8,128)S(1)} copy-done((f32[2,96,16,128]{3,2,1,0:T(8,128)S(1)}, f32[2,96,16,128]{3,2,1,0:T(8,128)}, u32[]{:S(2)}) %copy-start) | copy-done | bytes 1572888
  3.8 0.0 copy-start.2
  3.8 1.7 %copy-done.2 = f32[3,96,16,128]{3,2,1,0:T(8,128)S(1)} copy-done((f32[3,96,16,128]{3,2,1,0:T(8,128)S(1)}, f32[3,96,16,128]{3,2,1,0:T(8,128)}, u32[]{:S(2)}) %copy-start.2) | copy-done | bytes 2359320
  5.4 41.2 %supply.1 = (f32[16,16,16,128]{3,2,1,0:T(8,128)S(1)}, f32[96,16,128]{2,1,0:T(8,128)S(1)}, f32[2,2,16,128]{3,2,1,0:T(8,128)S(1)}, f32[2,2,96,128]{3,2,1,0:T(8,128)S(1)}, s32[8,8,128]{2,1,0:T(8,128)S(1)}) custom-call(s32[6,1]{1,0:T(8,128)S(1)} %copy.10.refs_0_, s32[1,1,8,2]{3,2,1,0:T(8,128)S(1)} %copy.11.refs_1_, s32[3,6,1]{2,1,0:T(8,128)S(1)} %copy.12.refs_2_, ...), custom_call_target="tpu_custom_call" | custom-call | tf_op jit(solution)/shard_map/supply/pallas_call | solution.py:451
  46.6 0.1 reshape.11.codes
  46.7 0.0 copy-done.3
  46.7 0.8 tangent.1
  47.5 8.5 %exchange_tangent.1 = (f32[3,16,128]{2,1,0:T(8,128)S(1)}, f32[3,112,128]{2,1,0:T(8,128)S(1)}) custom-call(f32[96,16,128]{2,1,0:T(8,128)S(1)} %get-tuple-element.31.refs_0_.field, f32[3,96,128]{2,1,0:T(8,128)S(1)} %get-tuple-element.32.refs_1_), custom_call_target="tpu_custom_call" | custom-call | tf_op jit(solution)/shard_map/exchange_tangent/pallas_call | solution.py:69
  56.0 10.1 %pull_push.1 = (f32[96,16,128]{2,1,0:T(8,128)S(1)}, f32[3,16,128]{2,1,0:T(8,128)S(1)}, f32[3,112,128]{2,1,0:T(8,128)S(1)}) custom-call(s32[16]{0:T(128)S(1)} %reshape.10.owners, s32[48]{0:T(128)S(1)} %reshape.11.codes, f32[96,16,128]{2,1,0:T(8,128)S(1)} %get-tuple-element.31.refs_0_.field, f32[3,16,128]{2,1,0:T(8,128)S(1)} %get-tuple-element.33.rows_in, ...), custom_call_target="tpu_custom_call" | custom-call | tf_op jit(solution)/shard_map/pull_push/pallas_call | solution.py:545
  66.2 8.4 %fold_late.1 = (f32[3,16,128]{2,1,0:T(8,128)S(1)}, f32[3,112,128]{2,1,0:T(8,128)S(1)}) custom-call(f32[3,16,128]{2,1,0:T(8,128)S(1)} %get-tuple-element.36.refs_0_, f32[3,112,128]{2,1,0:T(8,128)S(1)} %get-tuple-element.37.refs_1_), custom_call_target="tpu_custom_call" | custom-call | tf_op jit(solution)/shard_map/fold_late/pallas_call | solution.py:69
  74.5 0.9 outbox.1
  75.4 24.8 %exchange_adjoint.1.inbox = f32[16,16,16,128]{3,2,1,0:T(8,128)S(1)} custom-call(f32[16,16,16,128]{3,2,1,0:T(8,128)S(1)} %get-tuple-element.41.refs_0_), custom_call_target="tpu_custom_call" | custom-call | tf_op jit(solution)/shard_map/exchange_adjoint/pallas_call | solution.py:69
  100.2 0.0 copy-start.1
  100.2 6.0 %push.1 = (f32[96,16,128]{2,1,0:T(8,128)S(1)}, f32[3,16,128]{2,1,0:T(8,128)S(1)}, f32[3,112,128]{2,1,0:T(8,128)S(1)}) custom-call(s32[16]{0:T(128)S(1)} %reshape.10.owners, s32[48]{0:T(128)S(1)} %reshape.11.codes, f32[16,16,16,128]{3,2,1,0:T(8,128)S(1)} %exchange_adjoint.1.inbox), custom_call_target="tpu_custom_call" | custom-call | tf_op jit(solution)/shard_map/push/pallas_call | solution.py:545
  106.3 9.1 %fold_early.1 = (f32[3,16,128]{2,1,0:T(8,128)S(1)}, f32[3,112,128]{2,1,0:T(8,128)S(1)}) custom-call(f32[3,16,128]{2,1,0:T(8,128)S(1)} %get-tuple-element.43.refs_0_, f32[3,112,128]{2,1,0:T(8,128)S(1)} %get-tuple-element.44.refs_1_), custom_call_target="tpu_custom_call" | custom-call | tf_op jit(solution)/shard_map/fold_early/pallas_call | solution.py:69
  115.4 0.0 copy-done.1
  115.4 3.3 %force.1 = f32[3,96,16,128]{3,2,1,0:T(8,128)} custom-call(f32[2,96,16,128]{3,2,1,0:T(8,128)S(1)} %copy-done.1, f32[2,2,16,128]{3,2,1,0:T(8,128)S(1)} %get-tuple-element.26.rows_in, f32[2,2,96,128]{3,2,1,0:T(8,128)S(1)} %get-tuple-element.27.cols_in, f32[96,16,128]{2,1,0:T(8,128)S(1)} %get-tuple-element.40.later_adjoint, ...), custom_call_target="tpu_custom_call" | custom-call | tf_op jit(solution)/shard_map/force/pallas_call | solution.py:545
  (1 shorter events, 0.0 us)
Async XLA Ops:
  0.0 46.7 %copy-start.3 = (s32[6,1]{0,1:T(1,128)S(1)}, s32[6,1]{0,1:T(1,128)}, u32[]{:S(2)}) copy-start(s32[6,1]{0,1:T(1,128)} %param.7) | copy-start | bytes 76
  2.4 1.4 %copy-start = (f32[2,96,16,128]{3,2,1,0:T(8,128)S(1)}, f32[2,96,16,128]{3,2,1,0:T(8,128)}, u32[]{:S(2)}) copy-start(f32[2,96,16,128]{3,2,1,0:T(8,128)} %states.1) | copy-start | bytes 4718596
  3.8 1.7 %copy-start.2 = (f32[3,96,16,128]{3,2,1,0:T(8,128)S(1)}, f32[3,96,16,128]{3,2,1,0:T(8,128)}, u32[]{:S(2)}) copy-start(f32[3,96,16,128]{3,2,1,0:T(8,128)} %refs_4_.1) | copy-start | bytes 7077892
  100.2 15.2 %copy-start.1 = (f32[2,96,16,128]{3,2,1,0:T(8,128)S(1)}, f32[2,96,16,128]{3,2,1,0:T(8,128)}, u32[]{:S(2)}) copy-start(f32[2,96,16,128]{3,2,1,0:T(8,128)} %states.1) | copy-start | bytes 4718596

commit v3 on v2

v3 whole, which is shorter than its diff:
```python
import functools

import jax
import jax.numpy as jnp
from jax import lax
from jax.experimental import pallas as pl
from jax.experimental.pallas import tpu as pltpu
from jax.sharding import PartitionSpec as P

BX = 16
BY = 16
CAP = 2
QF = 8
STEPS = 2
STEP_SIZE = 1.0 / STEPS
WIN = BX + 3
CHUNK = 4
LANES = 24
VMEM_LIMIT = 40 * 1024 * 1024
F32 = jnp.float32


def shape(*dims):
    return jax.ShapeDtypeStruct(dims, F32)


def halo_plan(ins, outs):
    field, cols = ins
    rows_in, cols_in = outs
    rows = field.shape[0]
    main, low, high = pl.ds(8, rows), pl.ds(0, 8), pl.ds(rows + 8, 8)
    first, last = pl.ds(0, 8), pl.ds(rows - 8, 8)
    one, two = pl.ds(0, 1), pl.ds(1, 2)
    remote = [
        (cols.at[one], cols_in.at[one, main], 0, 1),
        (cols.at[two], cols_in.at[two, main], 0, -1),
        (field.at[pl.ds(rows - 1, 1)], rows_in.at[one], 1, 0),
        (field.at[pl.ds(0, 2)], rows_in.at[two], -1, 0),
        (cols.at[one, last], cols_in.at[one, low], 1, 1),
        (cols.at[one, first], cols_in.at[one, high], -1, 1),
        (cols.at[two, last], cols_in.at[two, low], 1, -1),
        (cols.at[two, first], cols_in.at[two, high], -1, -1),
    ]
    return remote


def fold_plan(ins, outs):
    rows_out, cols = ins
    rows_in, cols_in = outs
    rows = cols.shape[1] - 16
    main, low, high = pl.ds(8, rows), pl.ds(0, 8), pl.ds(rows + 8, 8)
    one, two = pl.ds(0, 1), pl.ds(1, 2)
    remote = [
        (cols.at[one, main], cols_in.at[one, main], 0, -1),
        (cols.at[two, main], cols_in.at[two, main], 0, 1),
        (rows_out.at[one], rows_in.at[one], -1, 0),
        (rows_out.at[two], rows_in.at[two], 1, 0),
        (cols.at[one, low], cols_in.at[one, high], -1, -1),
        (cols.at[one, high], cols_in.at[one, low], 1, -1),
        (cols.at[two, low], cols_in.at[two, high], -1, 1),
        (cols.at[two, high], cols_in.at[two, low], 1, 1),
    ]
    return remote


def cubic_weights(f):
    return (
        -f * (f - 1.0) * (f - 2.0) * (1.0 / 6.0),
        (f + 1.0) * (f - 1.0) * (f - 2.0) * 0.5,
        -(f + 1.0) * f * (f - 2.0) * 0.5,
        (f + 1.0) * f * (f - 1.0) * (1.0 / 6.0),
    )


def code_weights(u, v, q):
    depth_shift = lax.shift_right_logical(q, 3)
    fractions = [u, v, jnp.bitwise_and(q, QF - 1)]
    return depth_shift, [cubic_weights(f.astype(F32) * (1.0 / QF)) for f in fractions]


def weighted(weights, terms):
    total = weights[0] * terms[0]
    for weight, term in zip(weights[1:], terms[1:]):
        total = total + weight * term
    return total


def pull_rows(window, shift, weights):
    count, depth = window.shape[0] - 3, window.shape[2]
    rows = weighted(weights[0], [window[r : r + count] for r in range(4)])
    cols = weighted(
        weights[1],
        [(rows if t == 0 else pltpu.roll(rows, LANES - t, 1))[:, :BY] for t in range(4)],
    )
    base = pltpu.roll(cols, lax.rem(depth + 1 - shift, depth), 2)
    return weighted(
        weights[2], [base if m == 0 else pltpu.roll(base, depth - m, 2) for m in range(4)]
    )


def push_rows(values, shift, weights):
    count, _, depth = values.shape
    base = pltpu.roll(values, lax.rem(depth - 1 + shift, depth), 2)
    along = weighted(weights[2], [base if m == 0 else pltpu.roll(base, m, 2) for m in range(4)])
    wide = jnp.concatenate([along, jnp.zeros((count, LANES - BY, depth), F32)], axis=1)
    cols = weighted(weights[1], [wide if t == 0 else pltpu.roll(wide, t, 1) for t in range(4)])
    rows = []
    for i in range(count + 3):
        terms = [cols[i - r] * weights[0][r] for r in range(4) if 0 <= i - r < count]
        rows.append(sum(terms[1:], terms[0])[None])
    return jnp.concatenate(rows, axis=0)


def assemble(extended, field, rows_in, cols_in):
    rows = field.shape[0]
    extended[1 : rows + 1, 1 : BY + 1, :] = field[...]
    extended[0:1, 1 : BY + 1, :] = rows_in[0:1]
    extended[rows + 1 : rows + 3, 1 : BY + 1, :] = rows_in[1:3]
    for col, side in ((0, 0), (BY + 1, 1), (BY + 2, 2)):
        extended[:, col, :] = cols_in[side, 7 : rows + 10, :]


def emit_margins(total, acc, rows_out, cols_out):
    rows = total.shape[0]
    total[...] = acc[1 : rows + 1, 1 : BY + 1, :]
    rows_out[0:1] = acc[0:1, 1 : BY + 1, :]
    rows_out[1:3] = acc[rows + 1 : rows + 3, 1 : BY + 1, :]
    cols_out[...] = jnp.zeros_like(cols_out)
    for col, side in ((0, 0), (BY + 1, 1), (BY + 2, 2)):
        cols_out[side, 7 : rows + 10, :] = acc[:, col, :]


def gradient(states, rows_in, cols_in, step, block, blocks):
    rows, depth = states.shape[1], states.shape[3]
    first = block * BX
    cells = states[step, pl.ds(first, BX)]
    before = states[step, pl.ds(jnp.maximum(first - 1, 0), 1)]
    after = states[step, pl.ds(jnp.minimum(first + BX, rows - 1), 1)]
    before = jnp.where(block == 0, rows_in[0, pl.ds(step, 1)], before)
    after = jnp.where(block == blocks - 1, rows_in[1, pl.ds(step, 1)], after)
    left = cols_in[0, step, pl.ds(first, BX)][:, None, :]
    right = cols_in[1, step, pl.ds(first, BX)][:, None, :]
    col = lax.broadcasted_iota(jnp.int32, cells.shape, 1)
    below = jnp.concatenate([before, cells[:-1]], axis=0)
    above = jnp.concatenate([cells[1:], after], axis=0)
    lower = jnp.where(col == 0, left, pltpu.roll(cells, 1, 1))
    upper = jnp.where(col == BY - 1, right, pltpu.roll(cells, BY - 1, 1))
    return (
        (above - below) * 0.5,
        (upper - lower) * 0.5,
        (pltpu.roll(cells, depth - 1, 2) - pltpu.roll(cells, 1, 2)) * 0.5,
    )


def adjoints_kernel(
    n_gx, n_gy, plan, states, velocity,
    late_out, early_out, rows_out, cols_out,
    states_v, velocity_v, rows_v, cols_v, edge_cols, request, requested_v, requested_s,
    field, edges, halo_rows, halo_cols, extended, supplied, later_v, inbox,
    next_field, next_edges, next_rows, next_cols, running, sums, acc,
    total, late_margin_rows, late_margin_cols, late_fold_rows, late_fold_cols, late,
    outbox, returned, early_margin_rows, early_margin_cols, early_fold_rows, early_fold_cols,
    early, rank, order, sorted_owner, load_sem, send_sem, recv_sem, code_send, code_recv,
    brick_send, brick_recv, margin_send, margin_recv,
):
    gx, gy = lax.axis_index("gx"), lax.axis_index("gy")
    rows, depth = states.shape[1], states.shape[3]
    blocks, slots = rows // BX, n_gy * CAP

    def pull_of(k):
        return plan[k]

    def owner_of(slot):
        return plan[blocks + slot]

    def code_of(c, k):
        return plan[blocks + slots + c * blocks + k]

    def device(step_x, step_y):
        return (lax.rem(gx + step_x + n_gx, n_gx), lax.rem(gy + step_y + n_gy, n_gy))

    def remote(src, dst, send, recv, step_x, step_y):
        return pltpu.make_async_remote_copy(
            src_ref=src, dst_ref=dst, send_sem=send, recv_sem=recv,
            device_id=device(step_x, step_y), device_id_type=pl.DeviceIdType.MESH,
        )

    peers = [(i, j) for i in (-1, 1) for j in (-1, 0, 1)] + [(0, d) for d in range(1, n_gy)]
    barrier = pltpu.get_barrier_semaphore()
    for peer in peers:
        pl.semaphore_signal(
            barrier, inc=1, device_id=device(*peer), device_id_type=pl.DeviceIdType.MESH
        )
    loads = [
        pltpu.make_async_copy(states, states_v, load_sem.at[0]),
        pltpu.make_async_copy(velocity, velocity_v, load_sem.at[1]),
    ]
    for load in loads:
        load.start()
    peer_row = lax.broadcasted_iota(jnp.int32, request.shape, 0)
    entry = lax.broadcasted_iota(jnp.int32, request.shape, 1)
    lane = lax.broadcasted_iota(jnp.int32, request.shape, 2)
    place = jnp.where(entry < CAP, peer_row * CAP + entry, -1)
    table = jnp.zeros(request.shape, jnp.int32)
    for k in range(blocks):
        triple = jnp.where(
            lane == 0, code_of(0, k), jnp.where(lane == 1, code_of(1, k), code_of(2, k))
        )
        table = jnp.where(place == pull_of(k), triple, table)
    request[...] = table
    requested_v[pl.ds(gy, 1)] = request[pl.ds(gy, 1)]
    loads[0].wait()
    for step in range(STEPS):
        edge_cols[0, step] = states_v[step, :, BY - 1, :]
        edge_cols[1, step] = states_v[step, :, 0, :]
    pl.semaphore_wait(barrier, len(peers))

    copies = [
        remote(edge_cols.at[0], cols_v.at[0], send_sem.at[0], recv_sem.at[0], 0, 1),
        remote(edge_cols.at[1], cols_v.at[1], send_sem.at[1], recv_sem.at[1], 0, -1),
        remote(states_v.at[:, rows - 1], rows_v.at[0], send_sem.at[2], recv_sem.at[2], 1, 0),
        remote(states_v.at[:, 0], rows_v.at[1], send_sem.at[3], recv_sem.at[3], -1, 0),
    ]
    for copy in copies:
        copy.start()
    code_copies = []
    for d in range(1, n_gy):
        peer = lax.rem(gy + d, n_gy)
        code_copies.append(
            remote(request.at[peer], requested_v.at[gy], code_send.at[d], code_recv.at[d], 0, d)
        )
    for copy in code_copies:
        copy.start()
    loads[1].wait()
    for copy in copies:
        copy.wait()

    @pl.loop(0, blocks)
    def _(block):
        cells = pl.ds(block * BX, BX)
        terms = []
        for step in range(STEPS):
            parts = gradient(states_v, rows_v, cols_v, step, block, blocks)
            terms.append(
                (
                    velocity_v[0, cells] * parts[0]
                    + velocity_v[1, cells] * parts[1]
                    + velocity_v[2, cells] * parts[2]
                )
                * -STEP_SIZE
            )
        field[cells] = terms[0]
        for side, col in ((0, BY - 1), (1, 0), (2, 1)):
            edges[side, cells] = terms[0][:, col, :]
        later_v[cells] = terms[1]

    def margin_copies(phase, moves):
        copies = [
            remote(src, dst, margin_send.at[phase, i], margin_recv.at[phase, i], step_x, step_y)
            for i, (src, dst, step_x, step_y) in enumerate(moves)
        ]
        for copy in copies:
            copy.start()
        return copies

    copies = margin_copies(0, halo_plan((field, edges), (halo_rows, halo_cols)))
    saves = [
        pltpu.make_async_copy(rows_v, rows_out, load_sem.at[0]),
        pltpu.make_async_copy(cols_v, cols_out, load_sem.at[1]),
    ]
    for save in saves:
        save.start()
    for copy in code_copies:
        copy.wait()
    table_copy = pltpu.make_async_copy(requested_v, requested_s, load_sem.at[2])
    table_copy.start()
    table_copy.wait()
    for copy in copies:
        copy.wait()
    assemble(extended, field, halo_rows, halo_cols)

    def codes_of(slot):
        peer, e = lax.shift_right_logical(slot, 1), jnp.bitwise_and(slot, 1)
        return code_weights(*[requested_s[peer, e, c] for c in range(3)])

    def supply(peer, target):
        for e in range(CAP):
            slot = peer * CAP + e
            first = jnp.maximum(owner_of(slot), 0) * BX
            shift, weights = codes_of(slot)
            for row in range(0, BX, CHUNK):
                target[slot, row : row + CHUNK] = pull_rows(
                    extended[pl.ds(first + row, CHUNK + 3)], shift, weights
                )

    def brick_copy(phase, d, source, target):
        peer = lax.rem(gy + d, n_gy)
        return remote(
            source.at[pl.ds(peer * CAP, CAP)], target.at[pl.ds(gy * CAP, CAP)],
            brick_send.at[phase, d], brick_recv.at[phase, d], 0, d,
        )

    @pl.loop(1, n_gy)
    def _(d):
        supply(lax.rem(gy + d, n_gy), supplied)
        brick_copy(0, d, supplied, inbox).start()

    supply(gy, inbox)

    @pl.loop(0, slots)
    def _(s):
        mine = owner_of(s)

        def ahead(t, count):
            other = owner_of(t)
            before = jnp.logical_or(other < mine, jnp.logical_and(other == mine, t < s))
            return count + jnp.where(before, 1, 0)

        rank[s] = lax.fori_loop(0, slots, ahead, 0)

    @pl.loop(0, slots)
    def _(j):
        found = lax.fori_loop(0, slots, lambda t, at: jnp.where(rank[t] == j, t, at), 0)
        order[j] = found
        sorted_owner[j] = owner_of(found)

    for save in saves:
        save.wait()

    @pl.loop(1, n_gy)
    def _(d):
        brick_copy(0, d, supplied, inbox).wait()

    @pl.loop(0, blocks)
    def _(block):
        cells = pl.ds(block * BX, BX)
        values = inbox[pull_of(block)] + later_v[cells]
        next_field[cells] = values
        for side, col in ((0, BY - 1), (1, 0), (2, 1)):
            next_edges[side, cells] = values[:, col, :]

    for copy in margin_copies(1, halo_plan((next_field, next_edges), (next_rows, next_cols))):
        copy.wait()
    assemble(extended, next_field, next_rows, next_cols)

    def accumulate(values_of):
        running[...] = jnp.zeros_like(running)

        @pl.loop(0, slots)
        def _(j):
            slot, owner = order[j], sorted_owner[j]
            previous = sorted_owner[jnp.maximum(j - 1, 0)]
            running[...] = jnp.where(owner == previous, running[...], 0.0)
            shift, weights = codes_of(slot)
            first = jnp.maximum(owner, 0) * BX
            for row in range(0, BX, CHUNK):
                part = push_rows(values_of(slot, first, row, shift, weights), shift, weights)
                running[row : row + CHUNK + 3] = running[row : row + CHUNK + 3] + part
            sums[j] = running[...]

        acc[...] = jnp.zeros_like(acc)

        @pl.loop(0, blocks)
        def _(k):
            def at_most(t, count):
                return count + jnp.where(sorted_owner[t] <= k, 1, 0)

            last = jnp.maximum(lax.fori_loop(0, slots, at_most, 0) - 1, 0)
            window = pl.ds(k * BX, WIN)
            acc[window] = acc[window] + jnp.where(sorted_owner[last] == k, sums[last], 0.0)

    def fold_all(fold_rows, fold_cols, target):
        @pl.loop(0, blocks)
        def _(block):
            cells = pl.ds(block * BX, BX)
            target[cells] = fold(total[cells], fold_rows, fold_cols, block, blocks)

    def pulled(slot, first, row, shift, weights):
        return pull_rows(extended[pl.ds(first + row, CHUNK + 3)], shift, weights)

    accumulate(pulled)
    emit_margins(total, acc, late_margin_rows, late_margin_cols)
    moves = fold_plan((late_margin_rows, late_margin_cols), (late_fold_rows, late_fold_cols))
    for copy in margin_copies(2, moves):
        copy.wait()
    fold_all(late_fold_rows, late_fold_cols, late)
    late_save = pltpu.make_async_copy(late, late_out, load_sem.at[3])
    late_save.start()

    def fill(peer, target):
        for e in range(CAP):
            slot = peer * CAP + e
            brick = 0
            for k in range(1, blocks):
                brick = jnp.where(pull_of(k) == slot, k, brick)
            target[slot] = late[pl.ds(brick * BX, BX)]

    @pl.loop(1, n_gy)
    def _(d):
        fill(lax.rem(gy + d, n_gy), outbox)
        brick_copy(1, d, outbox, returned).start()

    fill(gy, returned)
    late_save.wait()

    @pl.loop(1, n_gy)
    def _(d):
        brick_copy(1, d, outbox, returned).wait()

    accumulate(lambda slot, first, row, shift, weights: returned[slot, row : row + CHUNK])
    emit_margins(total, acc, early_margin_rows, early_margin_cols)
    moves = fold_plan((early_margin_rows, early_margin_cols), (early_fold_rows, early_fold_cols))
    for copy in margin_copies(3, moves):
        copy.wait()
    fold_all(early_fold_rows, early_fold_cols, early)
    early_save = pltpu.make_async_copy(early, early_out, load_sem.at[4])
    early_save.start()
    early_save.wait()


def adjoints_call(states, velocity, plan):
    n_gx, n_gy = lax.axis_size("gx"), lax.axis_size("gy")
    _, rows, cols, depth = states.shape
    slots = n_gy * CAP
    table = (n_gy, 8, 128)
    hbm = pl.BlockSpec(memory_space=pltpu.HBM)
    dma = pltpu.SemaphoreType.DMA

    def vmem(*dims):
        return pltpu.VMEM(dims, F32)

    field = vmem(rows, cols, depth)
    edges = vmem(3, rows, depth)
    margin_rows, margin_cols = vmem(3, cols, depth), vmem(3, rows + 16, depth)
    extended = vmem(rows + 3, LANES, depth)
    bricks = vmem(slots, BX, BY, depth)
    margins = [margin_rows, margin_cols]
    return pl.pallas_call(
        lambda *refs: adjoints_kernel(n_gx, n_gy, *refs),
        name="adjoints",
        in_specs=[pl.BlockSpec(memory_space=pltpu.SMEM), hbm, hbm],
        out_specs=[hbm] * 4,
        out_shape=[
            shape(rows, cols, depth),
            shape(rows, cols, depth),
            shape(2, STEPS, cols, depth),
            shape(2, STEPS, rows, depth),
        ],
        scratch_shapes=[
            vmem(STEPS, rows, cols, depth),
            vmem(3, rows, cols, depth),
            vmem(2, STEPS, cols, depth),
            vmem(2, STEPS, rows, depth),
            vmem(2, STEPS, rows, depth),
            pltpu.VMEM(table, jnp.int32),
            pltpu.VMEM(table, jnp.int32),
            pltpu.SMEM(table, jnp.int32),
            field,
            edges,
            *margins,
            extended,
            bricks,
            field,
            bricks,
            field,
            edges,
            *margins,
            vmem(WIN, LANES, depth),
            vmem(slots, WIN, LANES, depth),
            extended,
            field,
            *margins,
            *margins,
            field,
            bricks,
            bricks,
            *margins,
            *margins,
            field,
            pltpu.SMEM((slots,), jnp.int32),
            pltpu.SMEM((slots,), jnp.int32),
            pltpu.SMEM((slots,), jnp.int32),
            dma((5,)),
            dma((4,)),
            dma((4,)),
            dma((n_gy,)),
            dma((n_gy,)),
            dma((2, n_gy)),
            dma((2, n_gy)),
            dma((4, 8)),
            dma((4, 8)),
        ],
        compiler_params=pltpu.CompilerParams(
            collective_id=0, has_side_effects=True, vmem_limit_bytes=VMEM_LIMIT
        ),
    )(plan, states, velocity)


def fold(values, rows_in, cols_in, block, blocks):
    depth = values.shape[2]
    is_first, is_last = block == 0, block == blocks - 1
    rows = cols_in.shape[1] - 16
    zeros = jnp.zeros((8, depth), F32)
    col = lax.broadcasted_iota(jnp.int32, values.shape, 1)
    row = lax.broadcasted_iota(jnp.int32, values.shape, 0)
    values = values + jnp.where(jnp.logical_and(is_last, row == BX - 1), rows_in[0:1], 0.0)
    for i in range(2):
        values = values + jnp.where(
            jnp.logical_and(is_first, row == i), rows_in[1 + i : 2 + i], 0.0
        )
    for side, place in ((0, BY - 1), (1, 0), (2, 1)):
        strip = cols_in[side, pl.ds(8 + block * BX, BX)]
        low = jnp.concatenate([cols_in[side, 0:8], zeros], axis=0)
        high = jnp.concatenate([zeros, cols_in[side, rows + 8 : rows + 16]], axis=0)
        strip = strip + jnp.where(is_first, low, 0.0) + jnp.where(is_last, high, 0.0)
        values = values + jnp.where(col == place, strip[:, None, :], 0.0)
    return values


def force_kernel(states, rows_in, cols_in, late_adjoint, early_adjoint, force):
    block, blocks = pl.program_id(0), pl.num_programs(0)
    scaled = [early_adjoint[...] * -STEP_SIZE, late_adjoint[...] * -STEP_SIZE]
    early = gradient(states, rows_in, cols_in, 0, block, blocks)
    late = gradient(states, rows_in, cols_in, 1, block, blocks)
    for c in range(3):
        force[c] = scaled[1] * late[c] + scaled[0] * early[c]


def whole(dims):
    return pl.BlockSpec(dims, lambda *_: (0,) * len(dims))


def body(velocity, states, pull_plan, send_plan, codes):
    _, rows, cols, depth = velocity.shape
    assert cols == BY and rows % BX == 0
    plan = jnp.concatenate([pull_plan.reshape(-1), send_plan.reshape(-1), codes.reshape(-1)])
    late_adjoint, early_adjoint, state_rows, state_cols = adjoints_call(states, velocity, plan)
    block = pl.BlockSpec((BX, BY, depth), lambda k: (k, 0, 0))
    return pl.pallas_call(
        force_kernel,
        name="force",
        grid=(rows // BX,),
        in_specs=[whole(states.shape), whole(state_rows.shape), whole(state_cols.shape)]
        + [block, block],
        out_specs=pl.BlockSpec((3, BX, BY, depth), lambda k: (0, k, 0, 0)),
        out_shape=shape(3, rows, cols, depth),
        compiler_params=pltpu.CompilerParams(vmem_limit_bytes=VMEM_LIMIT),
    )(states, state_rows, state_cols, late_adjoint, early_adjoint)


def solution(mesh):
    return jax.shard_map(
        body,
        mesh=mesh,
        in_specs=(
            P(None, "gx", "gy", None),
            P(None, "gx", "gy", None),
            P("gx", "gy"),
            P("gx", "gy", None, None),
            P(None, "gx", "gy"),
        ),
        out_specs=P(None, "gx", "gy", None),
        check_vma=False,
    )
```

time: 119 us -> 107 us (0.90)
  Pallas kernels: 113 us -> 101 us
  local copies, waits for them, and re-layouts: 5.55 us -> 4 us
  other arithmetic: 0 us -> 1.43 us
    pallas_call x10 -> x2, Pallas kernels: 113 us -> 101 us  [the longest x1 98.1 us: adjoints_call(): pl.pallas_call(lambda *refs: adjoints_kernel(n_gx, n_gy, *refs), name='ad...]
    unnamed x11 -> x7, local copies, waits for them, and re-layouts: 5.37 us -> 3.83 us
where the time goes in v3:
time: 107 us
  Pallas kernels  101 us (94%)
  local copies, waits for them, and re-layouts  4 us (4%)
  other arithmetic  1.43 us (1%)
    pallas_call x1, Pallas kernels, adjoints_call(): pl.pallas_call(lambda *refs: adjoints_kernel(n_gx, n_gy, *refs), name='ad...  98.1 us
    unnamed x7, local copies, waits for them, and re-layouts  3.83 us
    pallas_call x1, Pallas kernels, body(): pl.pallas_call(force_kernel, name='force', grid=(rows // BX,), in_specs=[...  3.29 us

profile of v3, /device:TPU:0, one launch (start us, length us, event | category | flops | bytes accessed | tf_op | source)
XLA Modules:
  0.0 106.8 jit_solution(17689120238533009656)
XLA Ops:
  0.0 0.7 reduce
  0.7 0.1 reshape.11
  0.8 0.8 copy.7
  1.5 0.1 reshape.10
  1.6 0.7 pad_add_fusion.refs_0_
  2.4 0.0 copy-start
  2.4 1.4 %copy-done = f32[2,96,16,128]{3,2,1,0:T(8,128)S(1)} copy-done((f32[2,96,16,128]{3,2,1,0:T(8,128)S(1)}, f32[2,96,16,128]{3,2,1,0:T(8,128)}, u32[]{:S(2)}) %copy-start) | copy-done | bytes 1572888
  3.8 0.0 copy-start.2
  3.8 1.7 %copy-done.2 = f32[3,96,16,128]{3,2,1,0:T(8,128)S(1)} copy-done((f32[3,96,16,128]{3,2,1,0:T(8,128)S(1)}, f32[3,96,16,128]{3,2,1,0:T(8,128)}, u32[]{:S(2)}) %copy-start.2) | copy-done | bytes 2359320
  5.4 0.0 copy-start.1
  5.4 98.1 %adjoints.1 = (f32[96,16,128]{2,1,0:T(8,128)S(1)}, f32[96,16,128]{2,1,0:T(8,128)S(1)}, f32[2,2,16,128]{3,2,1,0:T(8,128)S(1)}, f32[2,2,96,128]{3,2,1,0:T(8,128)S(1)}) custom-call(s32[40]{0:T(128)S(1)} %pad_add_fusion.refs_0_, f32[2,96,16,128]{3,2,1,0:T(8,128)S(1)} %copy-done, f32[3,96,16,128]{3,2,1,0:T(8,128)S(1)} %copy-done.2), custom_call_target="tpu_custom_call" | custom-call | tf_op jit(solution)/shard_map/adjoints/pallas_call | solution.py:438
  103.5 0.0 copy-done.1
  103.5 3.3 %force.1 = f32[3,96,16,128]{3,2,1,0:T(8,128)} custom-call(f32[2,96,16,128]{3,2,1,0:T(8,128)S(1)} %copy-done.1, f32[2,2,16,128]{3,2,1,0:T(8,128)S(1)} %get-tuple-element.9.rows_in, f32[2,2,96,128]{3,2,1,0:T(8,128)S(1)} %get-tuple-element.10.cols_in, f32[96,16,128]{2,1,0:T(8,128)S(1)} %get-tuple-element.11.late_adjoint, ...), custom_call_target="tpu_custom_call" | custom-call | tf_op jit(solution)/shard_map/force/pallas_call | solution.py:539
Async XLA Ops:
  2.4 1.4 %copy-start = (f32[2,96,16,128]{3,2,1,0:T(8,128)S(1)}, f32[2,96,16,128]{3,2,1,0:T(8,128)}, u32[]{:S(2)}) copy-start(f32[2,96,16,128]{3,2,1,0:T(8,128)} %states.1) | copy-start | bytes 4718596
  3.8 1.7 %copy-start.2 = (f32[3,96,16,128]{3,2,1,0:T(8,128)S(1)}, f32[3,96,16,128]{3,2,1,0:T(8,128)}, u32[]{:S(2)}) copy-start(f32[3,96,16,128]{3,2,1,0:T(8,128)} %refs_2_.1) | copy-start | bytes 7077892
  5.4 98.1 %copy-start.1 = (f32[2,96,16,128]{3,2,1,0:T(8,128)S(1)}, f32[2,96,16,128]{3,2,1,0:T(8,128)}, u32[]{:S(2)}) copy-start(f32[2,96,16,128]{3,2,1,0:T(8,128)} %states.1) | copy-start | bytes 4718596

commit v4 on v3

--- a/solution.py
+++ b/solution.py
@@ -16,7 +16,7 @@
 WIN = BX + 3
 CHUNK = 4
 LANES = 24
-VMEM_LIMIT = 40 * 1024 * 1024
+VMEM_LIMIT = 60 * 1024 * 1024
 F32 = jnp.float32
 
 
@@ -85,30 +85,59 @@
     return total
 
 
-def pull_rows(window, shift, weights):
-    count, depth = window.shape[0] - 3, window.shape[2]
+def pull_sides(window, weights):
+    count = window.shape[0] - 3
     rows = weighted(weights[0], [window[r : r + count] for r in range(4)])
-    cols = weighted(
+    return weighted(
         weights[1],
         [(rows if t == 0 else pltpu.roll(rows, LANES - t, 1))[:, :BY] for t in range(4)],
     )
-    base = pltpu.roll(cols, lax.rem(depth + 1 - shift, depth), 2)
+
+
+def pull_depth(values, shift, weights):
+    depth = values.shape[2]
+    base = pltpu.roll(values, lax.rem(depth + 1 - shift, depth), 2)
     return weighted(
         weights[2], [base if m == 0 else pltpu.roll(base, depth - m, 2) for m in range(4)]
     )
 
 
-def push_rows(values, shift, weights):
-    count, _, depth = values.shape
+def push_depth(values, shift, weights):
+    depth = values.shape[2]
     base = pltpu.roll(values, lax.rem(depth - 1 + shift, depth), 2)
-    along = weighted(weights[2], [base if m == 0 else pltpu.roll(base, m, 2) for m in range(4)])
-    wide = jnp.concatenate([along, jnp.zeros((count, LANES - BY, depth), F32)], axis=1)
-    cols = weighted(weights[1], [wide if t == 0 else pltpu.roll(wide, t, 1) for t in range(4)])
-    rows = []
-    for i in range(count + 3):
-        terms = [cols[i - r] * weights[0][r] for r in range(4) if 0 <= i - r < count]
-        rows.append(sum(terms[1:], terms[0])[None])
-    return jnp.concatenate(rows, axis=0)
+    return weighted(weights[2], [base if m == 0 else pltpu.roll(base, m, 2) for m in range(4)])
+
+
+def pull_push_depth(values, weights):
+    depth = values.shape[2]
+    w = weights[2]
+    total = (w[0] * w[0] + w[1] * w[1] + w[2] * w[2] + w[3] * w[3]) * values
+    for lag in range(1, 4):
+        tap = w[0] * w[lag]
+        for m in range(1, 4 - lag):
+            tap = tap + w[m] * w[m + lag]
+        total = total + tap * (pltpu.roll(values, lag, 2) + pltpu.roll(values, depth - lag, 2))
+    return total
+
+
+def push_sides(window, values_of, weights):
+    carry = None
+    for first in range(0, BX, CHUNK):
+        values = values_of(first)
+        depth = values.shape[2]
+        wide = jnp.concatenate([values, jnp.zeros((CHUNK, LANES - BY, depth), F32)], axis=1)
+        cols = weighted(weights[1], [wide if t == 0 else pltpu.roll(wide, t, 1) for t in range(4)])
+        rows = []
+        for i in range(CHUNK + 3):
+            terms = [cols[i - r] * weights[0][r] for r in range(4) if 0 <= i - r < CHUNK]
+            if carry is not None and i < 3:
+                terms.append(carry[i])
+            rows.append(sum(terms[1:], terms[0]))
+        for i in range(CHUNK):
+            window[first + i] = rows[i]
+        carry = rows[CHUNK:]
+    for i in range(3):
+        window[BX + i] = carry[i]
 
 
 def assemble(extended, field, rows_in, cols_in):
@@ -154,13 +183,13 @@
 
 def adjoints_kernel(
     n_gx, n_gy, plan, states, velocity,
-    late_out, early_out, rows_out, cols_out,
+    force,
     states_v, velocity_v, rows_v, cols_v, edge_cols, request, requested_v, requested_s,
     field, edges, halo_rows, halo_cols, extended, supplied, later_v, inbox,
-    next_field, next_edges, next_rows, next_cols, running, sums, acc,
+    next_field, next_edges, next_rows, next_cols, pushed, sums, acc,
     total, late_margin_rows, late_margin_cols, late_fold_rows, late_fold_cols, late,
     outbox, returned, early_margin_rows, early_margin_cols, early_fold_rows, early_fold_cols,
-    early, rank, order, sorted_owner, load_sem, send_sem, recv_sem, code_send, code_recv,
+    early_slopes, rank, order, sorted_owner, save_sem, load_sem, send_sem, recv_sem, code_send, code_recv,
     brick_send, brick_recv, margin_send, margin_recv,
 ):
     gx, gy = lax.axis_index("gx"), lax.axis_index("gy")
@@ -264,12 +293,6 @@
         return copies
 
     copies = margin_copies(0, halo_plan((field, edges), (halo_rows, halo_cols)))
-    saves = [
-        pltpu.make_async_copy(rows_v, rows_out, load_sem.at[0]),
-        pltpu.make_async_copy(cols_v, cols_out, load_sem.at[1]),
-    ]
-    for save in saves:
-        save.start()
     for copy in code_copies:
         copy.wait()
     table_copy = pltpu.make_async_copy(requested_v, requested_s, load_sem.at[2])
@@ -289,9 +312,8 @@
             first = jnp.maximum(owner_of(slot), 0) * BX
             shift, weights = codes_of(slot)
             for row in range(0, BX, CHUNK):
-                target[slot, row : row + CHUNK] = pull_rows(
-                    extended[pl.ds(first + row, CHUNK + 3)], shift, weights
-                )
+                sides = pull_sides(extended[pl.ds(first + row, CHUNK + 3)], weights)
+                target[slot, row : row + CHUNK] = pull_depth(sides, shift, weights)
 
     def brick_copy(phase, d, source, target):
         peer = lax.rem(gy + d, n_gy)
@@ -323,9 +345,6 @@
         found = lax.fori_loop(0, slots, lambda t, at: jnp.where(rank[t] == j, t, at), 0)
         order[j] = found
         sorted_owner[j] = owner_of(found)
-
-    for save in saves:
-        save.wait()
 
     @pl.loop(1, n_gy)
     def _(d):
@@ -343,20 +362,14 @@
         copy.wait()
     assemble(extended, next_field, next_rows, next_cols)
 
-    def accumulate(values_of):
-        running[...] = jnp.zeros_like(running)
+    def accumulate():
+        sums[0] = jnp.zeros(sums.shape[1:], F32)
 
         @pl.loop(0, slots)
         def _(j):
-            slot, owner = order[j], sorted_owner[j]
-            previous = sorted_owner[jnp.maximum(j - 1, 0)]
-            running[...] = jnp.where(owner == previous, running[...], 0.0)
-            shift, weights = codes_of(slot)
-            first = jnp.maximum(owner, 0) * BX
-            for row in range(0, BX, CHUNK):
-                part = push_rows(values_of(slot, first, row, shift, weights), shift, weights)
-                running[row : row + CHUNK + 3] = running[row : row + CHUNK + 3] + part
-            sums[j] = running[...]
+            before = jnp.maximum(j - 1, 0)
+            same = sorted_owner[j] == sorted_owner[before]
+            sums[j] = jnp.where(same, sums[before], 0.0) + pushed[order[j]]
 
         acc[...] = jnp.zeros_like(acc)
 
@@ -375,18 +388,23 @@
             cells = pl.ds(block * BX, BX)
             target[cells] = fold(total[cells], fold_rows, fold_cols, block, blocks)
 
-    def pulled(slot, first, row, shift, weights):
-        return pull_rows(extended[pl.ds(first + row, CHUNK + 3)], shift, weights)
-
-    accumulate(pulled)
+    @pl.loop(0, slots)
+    def _(slot):
+        first = jnp.maximum(owner_of(slot), 0) * BX
+        _, weights = codes_of(slot)
+
+        def values_of(row):
+            sides = pull_sides(extended[pl.ds(first + row, CHUNK + 3)], weights)
+            return pull_push_depth(sides, weights)
+
+        push_sides(pushed.at[slot], values_of, weights)
+
+    accumulate()
     emit_margins(total, acc, late_margin_rows, late_margin_cols)
     moves = fold_plan((late_margin_rows, late_margin_cols), (late_fold_rows, late_fold_cols))
     for copy in margin_copies(2, moves):
         copy.wait()
     fold_all(late_fold_rows, late_fold_cols, late)
-    late_save = pltpu.make_async_copy(late, late_out, load_sem.at[3])
-    late_save.start()
-
     def fill(peer, target):
         for e in range(CAP):
             slot = peer * CAP + e
@@ -401,21 +419,58 @@
         brick_copy(1, d, outbox, returned).start()
 
     fill(gy, returned)
-    late_save.wait()
+
+    @pl.loop(0, blocks)
+    def _(block):
+        cells = pl.ds(block * BX, BX)
+        scaled = late[cells] * -STEP_SIZE
+        parts = gradient(states_v, rows_v, cols_v, 1, block, blocks)
+        slopes = gradient(states_v, rows_v, cols_v, 0, block, blocks)
+        for c in range(3):
+            velocity_v[c, cells] = scaled * parts[c]
+            early_slopes[c, cells] = slopes[c]
+
+    def push(peer):
+        for e in range(CAP):
+            slot = peer * CAP + e
+            shift, weights = codes_of(slot)
+            push_sides(
+                pushed.at[slot],
+                lambda row: push_depth(returned[slot, row : row + CHUNK], shift, weights),
+                weights,
+            )
+
+    push(gy)
 
     @pl.loop(1, n_gy)
     def _(d):
         brick_copy(1, d, outbox, returned).wait()
-
-    accumulate(lambda slot, first, row, shift, weights: returned[slot, row : row + CHUNK])
+        push(lax.rem(gy + n_gy - d, n_gy))
+
+    accumulate()
     emit_margins(total, acc, early_margin_rows, early_margin_cols)
     moves = fold_plan((early_margin_rows, early_margin_cols), (early_fold_rows, early_fold_cols))
     for copy in margin_copies(3, moves):
         copy.wait()
-    fold_all(early_fold_rows, early_fold_cols, early)
-    early_save = pltpu.make_async_copy(early, early_out, load_sem.at[4])
-    early_save.start()
-    early_save.wait()
+
+    def save(block):
+        cells = pl.ds(block * BX, BX)
+        return pltpu.make_async_copy(
+            velocity_v.at[:, cells], force.at[:, cells], save_sem.at[block]
+        )
+
+    @pl.loop(0, blocks)
+    def _(block):
+        cells = pl.ds(block * BX, BX)
+        early = fold(total[cells], early_fold_rows, early_fold_cols, block, blocks)
+        scaled = early * -STEP_SIZE
+        for c in range(3):
+            velocity_v[c, cells] = velocity_v[c, cells] + scaled * early_slopes[c, cells]
+        save(block).start()
+
+    @pl.loop(0, blocks)
+    def _(block):
+        save(block).wait()
 
 
 def adjoints_call(states, velocity, plan):
@@ -439,13 +494,8 @@
         lambda *refs: adjoints_kernel(n_gx, n_gy, *refs),
         name="adjoints",
         in_specs=[pl.BlockSpec(memory_space=pltpu.SMEM), hbm, hbm],
-        out_specs=[hbm] * 4,
-        out_shape=[
-            shape(rows, cols, depth),
-            shape(rows, cols, depth),
-            shape(2, STEPS, cols, depth),
-            shape(2, STEPS, rows, depth),
-        ],
+        out_specs=hbm,
+        out_shape=shape(3, rows, cols, depth),
         scratch_shapes=[
             vmem(STEPS, rows, cols, depth),
             vmem(3, rows, cols, depth),
@@ -465,7 +515,7 @@
             field,
             edges,
             *margins,
-            vmem(WIN, LANES, depth),
+            vmem(slots, WIN, LANES, depth),
             vmem(slots, WIN, LANES, depth),
             extended,
             field,
@@ -476,11 +526,12 @@
             bricks,
             *margins,
             *margins,
-            field,
+            vmem(3, rows, cols, depth),
             pltpu.SMEM((slots,), jnp.int32),
             pltpu.SMEM((slots,), jnp.int32),
             pltpu.SMEM((slots,), jnp.int32),
-            dma((5,)),
+            dma((rows // BX,)),
+            dma((3,)),
             dma((4,)),
             dma((4,)),
             dma((n_gy,)),
@@ -517,35 +568,11 @@
     return values
 
 
-def force_kernel(states, rows_in, cols_in, late_adjoint, early_adjoint, force):
-    block, blocks = pl.program_id(0), pl.num_programs(0)
-    scaled = [early_adjoint[...] * -STEP_SIZE, late_adjoint[...] * -STEP_SIZE]
-    early = gradient(states, rows_in, cols_in, 0, block, blocks)
-    late = gradient(states, rows_in, cols_in, 1, block, blocks)
-    for c in range(3):
-        force[c] = scaled[1] * late[c] + scaled[0] * early[c]
-
-
-def whole(dims):
-    return pl.BlockSpec(dims, lambda *_: (0,) * len(dims))
-
-
 def body(velocity, states, pull_plan, send_plan, codes):
     _, rows, cols, depth = velocity.shape
     assert cols == BY and rows % BX == 0
     plan = jnp.concatenate([pull_plan.reshape(-1), send_plan.reshape(-1), codes.reshape(-1)])
-    late_adjoint, early_adjoint, state_rows, state_cols = adjoints_call(states, velocity, plan)
-    block = pl.BlockSpec((BX, BY, depth), lambda k: (k, 0, 0))
-    return pl.pallas_call(
-        force_kernel,
-        name="force",
-        grid=(rows // BX,),
-        in_specs=[whole(states.shape), whole(state_rows.shape), whole(state_cols.shape)]
-        + [block, block],
-        out_specs=pl.BlockSpec((3, BX, BY, depth), lambda k: (0, k, 0, 0)),
-        out_shape=shape(3, rows, cols, depth),
-        compiler_params=pltpu.CompilerParams(vmem_limit_bytes=VMEM_LIMIT),
-    )(states, state_rows, state_cols, late_adjoint, early_adjoint)
+    return adjoints_call(states, velocity, plan)
 
 
 def solution(mesh):

time: 107 us -> 101 us (0.944)
  Pallas kernels: 101 us -> 95.2 us
    pallas_call x1 -> x0, Pallas kernels: 3.29 us -> none  [body(): pl.pallas_call(force_kernel, name='force', grid=(rows // BX,), in_specs=[...]
    pallas_call x1, Pallas kernels: 98.1 us -> 95.2 us  [adjoints_call(): pl.pallas_call(lambda *refs: adjoints_kernel(n_gx, n_gy, *refs), name='ad...]
    unnamed x7 -> x2, local copies, waits for them, and re-layouts: 3.83 us -> 3.98 us
where the time goes in v4:
time: 101 us
  Pallas kernels  95.2 us (94%)
  local copies, waits for them, and re-layouts  4.14 us (4%)
  other arithmetic  1.94 us (2%)
    pallas_call x1, Pallas kernels, adjoints_call(): pl.pallas_call(lambda *refs: adjoints_kernel(n_gx, n_gy, *refs), name='ad...  95.2 us
    unnamed x2, local copies, waits for them, and re-layouts  3.98 us

profile of v4, /device:TPU:0, one launch (start us, length us, event | category | flops | bytes accessed | tf_op | source)
XLA Modules:
  0.0 101.3 jit_solution(6292000900915244790)
XLA Ops:
  0.0 0.7 reduce
  0.7 0.1 reshape.11
  0.8 0.8 copy.7
  1.5 0.1 reshape.10
  1.6 1.2 %pad_add_fusion.refs_0_ = s32[40]{0:T(128)} fusion(s32[18]{0:T(128)S(1)} %reshape.11, s32[16]{0:T(128)S(1)} %reshape.10, s32[6]{0:T(128)} %bitcast.3), kind=kLoop, calls=%fused_computation | loop fusion | flops 80 | bytes 320 | tf_op jit(solution)/shard_map/concatenate | solution.py:574
  2.9 95.2 %adjoints.1 = f32[3,96,16,128]{3,2,1,0:T(8,128)} custom-call(s32[40]{0:T(128)} %pad_add_fusion.refs_0_, f32[2,96,16,128]{3,2,1,0:T(8,128)} %refs_1_.1, f32[3,96,16,128]{3,2,1,0:T(8,128)} %refs_2_.1), custom_call_target="tpu_custom_call" | custom-call | tf_op jit(solution)/shard_map/adjoints/pallas_call | solution.py:493
  98.0 3.2 %copy.9 = f32[3,96,16,128]{3,2,1,0:T(8,128)} copy(f32[3,96,16,128]{3,2,1,0:T(8,128)} %adjoints.1) | data formatting | bytes 4718592

commit v5 on v4

--- a/solution.py
+++ b/solution.py
@@ -108,16 +108,14 @@
     return weighted(weights[2], [base if m == 0 else pltpu.roll(base, m, 2) for m in range(4)])
 
 
-def pull_push_depth(values, weights):
-    depth = values.shape[2]
-    w = weights[2]
-    total = (w[0] * w[0] + w[1] * w[1] + w[2] * w[2] + w[3] * w[3]) * values
-    for lag in range(1, 4):
+def correlated(w):
+    taps = []
+    for lag in range(4):
         tap = w[0] * w[lag]
         for m in range(1, 4 - lag):
             tap = tap + w[m] * w[m + lag]
-        total = total + tap * (pltpu.roll(values, lag, 2) + pltpu.roll(values, depth - lag, 2))
-    return total
+        taps.append(tap)
+    return taps
 
 
 def push_sides(window, values_of, weights):
@@ -182,14 +180,14 @@
 
 
 def adjoints_kernel(
-    n_gx, n_gy, plan, states, velocity,
+    n_gx, n_gy, pulls, owners, codes, states, velocity,
     force,
     states_v, velocity_v, rows_v, cols_v, edge_cols, request, requested_v, requested_s,
     field, edges, halo_rows, halo_cols, extended, supplied, later_v, inbox,
     next_field, next_edges, next_rows, next_cols, pushed, sums, acc,
     total, late_margin_rows, late_margin_cols, late_fold_rows, late_fold_cols, late,
     outbox, returned, early_margin_rows, early_margin_cols, early_fold_rows, early_fold_cols,
-    early_slopes, rank, order, sorted_owner, save_sem, load_sem, send_sem, recv_sem, code_send, code_recv,
+    early_slopes, brick, taps_high, taps_low, kept, rank, order, sorted_owner, save_sem, load_sem, send_sem, recv_sem, code_send, code_recv,
     brick_send, brick_recv, margin_send, margin_recv,
 ):
     gx, gy = lax.axis_index("gx"), lax.axis_index("gy")
@@ -197,13 +195,13 @@
     blocks, slots = rows // BX, n_gy * CAP
 
     def pull_of(k):
-        return plan[k]
+        return pulls[k]
 
     def owner_of(slot):
-        return plan[blocks + slot]
+        return owners[0, 0, jnp.bitwise_and(slot, 1), lax.shift_right_logical(slot, 1)]
 
     def code_of(c, k):
-        return plan[blocks + slots + c * blocks + k]
+        return codes[c, 0, k]
 
     def device(step_x, step_y):
         return (lax.rem(gx + step_x + n_gx, n_gx), lax.rem(gy + step_y + n_gy, n_gy))
@@ -331,6 +329,38 @@
 
     @pl.loop(0, slots)
     def _(s):
+        _, weights = codes_of(s)
+        for axis in range(3):
+            for m in range(4):
+                kept[s, 4 * axis + m] = weights[axis][m]
+        taps = correlated(weights[2])
+        row = lax.broadcasted_iota(jnp.int32, (depth, depth), 0)
+        col = lax.broadcasted_iota(jnp.int32, (depth, depth), 1)
+        gap = jnp.abs(row - col)
+        gap = jnp.minimum(gap, depth - gap)
+        matrix = jnp.zeros((depth, depth), F32)
+        for lag in range(4):
+            matrix = jnp.where(gap == lag, taps[lag], matrix)
+        high = matrix.astype(jnp.bfloat16)
+        taps_high[s] = high
+        taps_low[s] = (matrix - high.astype(F32)).astype(jnp.bfloat16)
+
+    def kept_weights(slot):
+        return [[kept[slot, 4 * axis + m] for m in range(4)] for axis in range(3)]
+
+    def correlate(slot, values):
+        high = values.astype(jnp.bfloat16)
+        low = (values - high.astype(F32)).astype(jnp.bfloat16)
+
+        def dot(left, right):
+            return jnp.dot(left, right, preferred_element_type=F32)
+
+        return (
+            dot(high, taps_low[slot]) + dot(low, taps_high[slot]) + dot(high, taps_high[slot])
+        )
+
+    @pl.loop(0, slots)
+    def _(s):
         mine = owner_of(s)
 
         def ahead(t, count):
@@ -391,13 +421,14 @@
     @pl.loop(0, slots)
     def _(slot):
         first = jnp.maximum(owner_of(slot), 0) * BX
-        _, weights = codes_of(slot)
-
-        def values_of(row):
-            sides = pull_sides(extended[pl.ds(first + row, CHUNK + 3)], weights)
-            return pull_push_depth(sides, weights)
-
-        push_sides(pushed.at[slot], values_of, weights)
+        weights = kept_weights(slot)
+        for row in range(0, BX, CHUNK):
+            brick[row : row + CHUNK] = pull_sides(
+                extended[pl.ds(first + row, CHUNK + 3)], weights
+            )
+        values = correlate(slot, brick[...].reshape(BX * BY, depth))
+        brick[...] = values.reshape(BX, BY, depth)
+        push_sides(pushed.at[slot], lambda row: brick[row : row + CHUNK], weights)
 
     accumulate()
     emit_margins(total, acc, late_margin_rows, late_margin_cols)
@@ -408,10 +439,10 @@
     def fill(peer, target):
         for e in range(CAP):
             slot = peer * CAP + e
-            brick = 0
+            source = 0
             for k in range(1, blocks):
-                brick = jnp.where(pull_of(k) == slot, k, brick)
-            target[slot] = late[pl.ds(brick * BX, BX)]
+                source = jnp.where(pull_of(k) == slot, k, source)
+            target[slot] = late[pl.ds(source * BX, BX)]
 
     @pl.loop(1, n_gy)
     def _(d):
@@ -433,7 +464,9 @@
     def push(peer):
         for e in range(CAP):
             slot = peer * CAP + e
-            shift, weights = codes_of(slot)
+            peer_row, e_row = lax.shift_right_logical(slot, 1), jnp.bitwise_and(slot, 1)
+            shift = lax.shift_right_logical(requested_s[peer_row, e_row, 2], 3)
+            weights = kept_weights(slot)
             push_sides(
                 pushed.at[slot],
                 lambda row: push_depth(returned[slot, row : row + CHUNK], shift, weights),
@@ -473,7 +506,7 @@
         save(block).wait()
 
 
-def adjoints_call(states, velocity, plan):
+def adjoints_call(states, velocity, pulls, owners, codes):
     n_gx, n_gy = lax.axis_size("gx"), lax.axis_size("gy")
     _, rows, cols, depth = states.shape
     slots = n_gy * CAP
@@ -493,7 +526,7 @@
     return pl.pallas_call(
         lambda *refs: adjoints_kernel(n_gx, n_gy, *refs),
         name="adjoints",
-        in_specs=[pl.BlockSpec(memory_space=pltpu.SMEM), hbm, hbm],
+        in_specs=[pl.BlockSpec(memory_space=pltpu.SMEM)] * 3 + [hbm, hbm],
         out_specs=hbm,
         out_shape=shape(3, rows, cols, depth),
         scratch_shapes=[
@@ -527,6 +560,10 @@
             *margins,
             *margins,
             vmem(3, rows, cols, depth),
+            vmem(BX, BY, depth),
+            pltpu.VMEM((slots, depth, depth), jnp.bfloat16),
+            pltpu.VMEM((slots, depth, depth), jnp.bfloat16),
+            pltpu.SMEM((slots, 12), F32),
             pltpu.SMEM((slots,), jnp.int32),
             pltpu.SMEM((slots,), jnp.int32),
             pltpu.SMEM((slots,), jnp.int32),
@@ -544,7 +581,7 @@
         compiler_params=pltpu.CompilerParams(
             collective_id=0, has_side_effects=True, vmem_limit_bytes=VMEM_LIMIT
         ),
-    )(plan, states, velocity)
+    )(pulls, owners, codes, states, velocity)
 
 
 def fold(values, rows_in, cols_in, block, blocks):
@@ -571,8 +608,13 @@
 def body(velocity, states, pull_plan, send_plan, codes):
     _, rows, cols, depth = velocity.shape
     assert cols == BY and rows % BX == 0
-    plan = jnp.concatenate([pull_plan.reshape(-1), send_plan.reshape(-1), codes.reshape(-1)])
-    return adjoints_call(states, velocity, plan)
+    return adjoints_call(
+        states,
+        velocity,
+        pull_plan.reshape(rows // BX),
+        send_plan.transpose(0, 1, 3, 2),
+        codes.transpose(0, 2, 1),
+    )
 
 
 def solution(mesh):

time: 101 us -> 98.6 us (0.976)
  other arithmetic: 1.94 us -> 0 us
    concatenate x1 -> x0, other arithmetic: 1.24 us -> none  [body(): jnp.concatenate([pull_plan.reshape(-1), send_plan.reshape(-1), codes.resh...]
    unnamed x2 -> x1, local copies, waits for them, and re-layouts: 3.98 us -> 3.22 us
where the time goes in v5:
time: 98.6 us; the launch traced here: 98.5 us
  Pallas kernels  95.2 us (97%)
  local copies, waits for them, and re-layouts  3.22 us (3%)
    pallas_call x1, Pallas kernels, adjoints_call(): pl.pallas_call(lambda *refs: adjoints_kernel(n_gx, n_gy, *refs), name='ad...  95.2 us
    unnamed x1, local copies, waits for them, and re-layouts  3.22 us

profile of v5, /device:TPU:0, one launch (start us, length us, event | category | flops | bytes accessed | tf_op | source)
XLA Modules:
  0.0 98.5 jit_solution(17710937028688887172)
XLA Ops:
  0.0 95.2 %adjoints.1 = f32[3,96,16,128]{3,2,1,0:T(8,128)} custom-call(s32[6]{0:T(128)} %bitcast.5, s32[1,1,2,8]{3,2,1,0:T(2,128)} %bitcast.4, s32[3,1,6]{2,1,0:T(1,128)} %bitcast.3, f32[2,96,16,128]{3,2,1,0:T(8,128)} %refs_3_.1, f32[3,96,16,128]{3,2,1,0:T(8,128)} %refs_4_.1), custom_call_target="tpu_custom_call" | custom-call | tf_op jit(solution)/shard_map/adjoints/pallas_call | solution.py:526
  95.2 3.2 %copy.7 = f32[3,96,16,128]{3,2,1,0:T(8,128)} copy(f32[3,96,16,128]{3,2,1,0:T(8,128)} %adjoints.1) | data formatting | bytes 4718592

commit v6 on v5

--- a/solution.py
+++ b/solution.py
@@ -444,9 +444,15 @@
                 source = jnp.where(pull_of(k) == slot, k, source)
             target[slot] = late[pl.ds(source * BX, BX)]
 
+    wave = n_gy // 2
+    rest = n_gy - wave
+
     @pl.loop(1, n_gy)
     def _(d):
         fill(lax.rem(gy + d, n_gy), outbox)
+
+    @pl.loop(1, wave + 1)
+    def _(d):
         brick_copy(1, d, outbox, returned).start()
 
     fill(gy, returned)
@@ -473,9 +479,19 @@
                 weights,
             )
 
+    @pl.loop(1, rest)
+    def _(d):
+        brick_copy(1, d, outbox, returned).wait_send()
+        brick_copy(1, d + wave, outbox, returned).start()
+
     push(gy)
 
-    @pl.loop(1, n_gy)
+    @pl.loop(1, rest)
+    def _(d):
+        brick_copy(1, d, outbox, returned).wait_recv()
+        push(lax.rem(gy + n_gy - d, n_gy))
+
+    @pl.loop(rest, n_gy)
     def _(d):
         brick_copy(1, d, outbox, returned).wait()
         push(lax.rem(gy + n_gy - d, n_gy))

time: 98.6 us -> 98.8 us (level)
  no operation moved by 1% of the time
where the time goes in v6:
time: 98.8 us; the launch traced here: 98.7 us
  Pallas kernels  95.4 us (97%)
  local copies, waits for them, and re-layouts  3.22 us (3%)
    pallas_call x1, Pallas kernels, adjoints_call(): pl.pallas_call(lambda *refs: adjoints_kernel(n_gx, n_gy, *refs), name='ad...  95.4 us
    unnamed x1, local copies, waits for them, and re-layouts  3.22 us

profile of v6, /device:TPU:0, one launch (start us, length us, event | category | flops | bytes accessed | tf_op | source)
XLA Modules:
  0.0 98.7 jit_solution(11504054324482760335)
XLA Ops:
  0.0 95.4 %adjoints.1 = f32[3,96,16,128]{3,2,1,0:T(8,128)} custom-call(s32[6]{0:T(128)} %bitcast.5, s32[1,1,2,8]{3,2,1,0:T(2,128)} %bitcast.4, s32[3,1,6]{2,1,0:T(1,128)} %bitcast.3, f32[2,96,16,128]{3,2,1,0:T(8,128)} %refs_3_.1, f32[3,96,16,128]{3,2,1,0:T(8,128)} %refs_4_.1), custom_call_target="tpu_custom_call" | custom-call | tf_op jit(solution)/shard_map/adjoints/pallas_call | solution.py:542
  95.4 3.2 %copy.7 = f32[3,96,16,128]{3,2,1,0:T(8,128)} copy(f32[3,96,16,128]{3,2,1,0:T(8,128)} %adjoints.1) | data formatting | bytes 4718592

commit v7 on v5

--- a/solution.py
+++ b/solution.py
@@ -140,7 +140,6 @@
 
 def assemble(extended, field, rows_in, cols_in):
     rows = field.shape[0]
-    extended[1 : rows + 1, 1 : BY + 1, :] = field[...]
     extended[0:1, 1 : BY + 1, :] = rows_in[0:1]
     extended[rows + 1 : rows + 3, 1 : BY + 1, :] = rows_in[1:3]
     for col, side in ((0, 0), (BY + 1, 1), (BY + 2, 2)):
@@ -149,7 +148,6 @@
 
 def emit_margins(total, acc, rows_out, cols_out):
     rows = total.shape[0]
-    total[...] = acc[1 : rows + 1, 1 : BY + 1, :]
     rows_out[0:1] = acc[0:1, 1 : BY + 1, :]
     rows_out[1:3] = acc[rows + 1 : rows + 3, 1 : BY + 1, :]
     cols_out[...] = jnp.zeros_like(cols_out)
@@ -296,6 +294,7 @@
     table_copy = pltpu.make_async_copy(requested_v, requested_s, load_sem.at[2])
     table_copy.start()
     table_copy.wait()
+    extended[1 : rows + 1, 1 : BY + 1, :] = field[...]
     for copy in copies:
         copy.wait()
     assemble(extended, field, halo_rows, halo_cols)
@@ -388,7 +387,9 @@
         for side, col in ((0, BY - 1), (1, 0), (2, 1)):
             next_edges[side, cells] = values[:, col, :]
 
-    for copy in margin_copies(1, halo_plan((next_field, next_edges), (next_rows, next_cols))):
+    copies = margin_copies(1, halo_plan((next_field, next_edges), (next_rows, next_cols)))
+    extended[1 : rows + 1, 1 : BY + 1, :] = next_field[...]
+    for copy in copies:
         copy.wait()
     assemble(extended, next_field, next_rows, next_cols)
 
@@ -433,7 +434,9 @@
     accumulate()
     emit_margins(total, acc, late_margin_rows, late_margin_cols)
     moves = fold_plan((late_margin_rows, late_margin_cols), (late_fold_rows, late_fold_cols))
-    for copy in margin_copies(2, moves):
+    copies = margin_copies(2, moves)
+    total[...] = acc[1 : rows + 1, 1 : BY + 1, :]
+    for copy in copies:
         copy.wait()
     fold_all(late_fold_rows, late_fold_cols, late)
     def fill(peer, target):
@@ -483,7 +486,9 @@
     accumulate()
     emit_margins(total, acc, early_margin_rows, early_margin_cols)
     moves = fold_plan((early_margin_rows, early_margin_cols), (early_fold_rows, early_fold_cols))
-    for copy in margin_copies(3, moves):
+    copies = margin_copies(3, moves)
+    total[...] = acc[1 : rows + 1, 1 : BY + 1, :]
+    for copy in copies:
         copy.wait()
 
     def save(block):

time: 98.6 us -> 98.4 us (level)
  no operation moved by 1% of the time
where the time goes in v7:
time: 98.4 us; the launch traced here: 98.2 us
  Pallas kernels  95 us (97%)
  local copies, waits for them, and re-layouts  3.22 us (3%)
    pallas_call x1, Pallas kernels, adjoints_call(): pl.pallas_call(lambda *refs: adjoints_kernel(n_gx, n_gy, *refs), name='ad...  95 us
    unnamed x1, local copies, waits for them, and re-layouts  3.22 us

profile of v7, /device:TPU:0, one launch (start us, length us, event | category | flops | bytes accessed | tf_op | source)
XLA Modules:
  0.0 98.2 jit_solution(18170436083757278494)
XLA Ops:
  0.0 95.0 %adjoints.1 = f32[3,96,16,128]{3,2,1,0:T(8,128)} custom-call(s32[6]{0:T(128)} %bitcast.5, s32[1,1,2,8]{3,2,1,0:T(2,128)} %bitcast.4, s32[3,1,6]{2,1,0:T(1,128)} %bitcast.3, f32[2,96,16,128]{3,2,1,0:T(8,128)} %refs_3_.1, f32[3,96,16,128]{3,2,1,0:T(8,128)} %refs_4_.1), custom_call_target="tpu_custom_call" | custom-call | tf_op jit(solution)/shard_map/adjoints/pallas_call | solution.py:531
  95.0 3.2 %copy.7 = f32[3,96,16,128]{3,2,1,0:T(8,128)} copy(f32[3,96,16,128]{3,2,1,0:T(8,128)} %adjoints.1) | data formatting | bytes 4718592
